TPU v7x, 128 devices: a whole 4x4x4 slice. The times are simulated.
128 devices in a mesh: seq: 64 (over x_lo, z, y, core), head: 2 (over x_hi).
Axes of the slice: x: 4 (x_hi: 2, x_lo: 2; x = x_hi * 2 + x_lo), y: 4, z: 4, core: 2. Of those that a mesh axis runs over, the one named last changes fastest.
Arguments:
- video_query: bfloat16 [131072, 2048], P('seq', 'head'), may hold values from -360 to 360
- video_kv: bfloat16 [2, 131072, 2048], P(None, 'seq', 'head'), may hold values from -360 to 360
- video_clip: int32 [131072], P('seq'), may hold values from 0 to 7, never falling along the last dimension, each value on 1 to 98304 neighbouring positions
- audio_hidden: bfloat16 [256, 2048], replicated, may hold values from -6 to 6
- audio_qkv_weight: bfloat16 [64, 128, 1536], P('seq', None, 'head'), may hold values from -0.125 to 0.125
- audio_clip: int32 [256], replicated, may hold values from 0 to 7, never falling along the last dimension, each value on 1 to 192 neighbouring positions
- audio_out_weight: bfloat16 [2048, 2048], P('head', 'seq'), may hold values from -0.125 to 0.125
Outputs:
- video_attn: bfloat16 [131072, 2048], P('seq', 'head')
- audio_out: bfloat16 [256, 2048], P('head', 'seq')
Inputs may be any that keep to these rules, and one draw needn't show every extreme that they name: `video_clip`: rows of one clip are consecutive; every clip number appears among the video rows. `audio_clip`: rows of one clip are consecutive; every clip number appears among the audio rows.
All inputs are finite; a program needn't handle non-finite values.
Results may differ from a plain program's by a relative error of at most 0.009.
The roundings to bfloat16 on the way count: a program that leaves them out, or rounds other values in their place, can miss the bound.
Values may be sent and summed in bfloat16 or wider, within the bound.
A program may use at most 128 MiB of HBM per device.

v0:
```python
import math

import jax
import jax.numpy as jnp
from jax import lax
from jax.sharding import Mesh
from jax.sharding import PartitionSpec as P

HD = 64
SEQ = ("seq_0", "seq_1", "seq_2", "seq_3")


NEG = -1e30


def in_blocks(x, dim, devices):
    before, after = (x.shape[:dim], x.shape[dim + 1 :])
    return jnp.moveaxis(x.reshape(*before, devices, -1, *after), dim, 0)


def summed_on_arrival(x, axis, dim):
    blocks = in_blocks(x, dim, lax.axis_size(axis))
    arrived = lax.all_to_all(blocks, axis, split_axis=0, concat_axis=0, tiled=True)
    return arrived.sum(axis=0)


def summed_rows(x, axes, dim):
    far, near = axes
    blocks = in_blocks(x, dim, lax.axis_size(far))
    nearer = summed_on_arrival(blocks, near, dim + 1)
    arrived = lax.all_to_all(nearer, far, split_axis=0, concat_axis=0, tiled=True)
    return arrived.sum(axis=0)


def filled_up(lines, devices):
    spare = -lines.shape[0] % devices
    if not spare:
        return lines
    return jnp.concatenate([lines, jnp.zeros((spare, *lines.shape[1:]), lines.dtype)])


def copy_for_each(x, axis):
    devices = lax.axis_size(axis)
    return lax.all_to_all(jnp.broadcast_to(x[None], (devices, *x.shape)), axis, 0, 0, tiled=True)


def laid_out(blocks, dim):
    shape = list(blocks.shape[1:])
    shape[dim] *= blocks.shape[0]
    return jnp.moveaxis(blocks, 0, dim).reshape(shape)


def whole_of(x, axes, dim):
    far, near = axes
    initial = copy_for_each(x, far)
    blocks = jnp.swapaxes(copy_for_each(initial, near), 0, 1)
    return laid_out(blocks.reshape(-1, *x.shape), dim)


def sum_by_parts(x, axes):
    lines = x.reshape(-1, x.shape[-1])
    own = summed_rows(filled_up(lines, lax.axis_size(axes[0]) * lax.axis_size(axes[1])), axes, 0)
    whole = whole_of(own, axes, 0)
    return whole[: len(lines)].reshape(x.shape)


def of_everyone(x, axis):
    everything = copy_for_each(x, axis)
    return jnp.max(everything, axis=0)


def sent_together(arrays, axis, dim, along):
    both = jnp.concatenate(arrays, axis=along)
    filled, at, done = (summed_rows(both, axis, dim), 0, [])
    for a in arrays:
        done.append(lax.slice_in_dim(filled, at, at + a.shape[along], axis=along))
        at += a.shape[along]
    return tuple(done)


def gathered_copies(x, axis, dim):
    return laid_out(copy_for_each(x, axis), dim)


def shards(
    video_query, video_kv, video_clip, audio_hidden, audio_qkv_weight, audio_clip, audio_out_weight
):
    audio_rows = audio_hidden.shape[0]
    width = video_query.shape[1]
    heads = width // HD
    local_rows = video_query.shape[0]
    block = math.gcd(local_rows, 512)
    blocks = local_rows // block
    quarters = lax.axis_size(SEQ) // 16
    position = lax.axis_index(SEQ)
    feature_group = position % 16
    quarter = position // 16
    local_weight = audio_qkv_weight[0]
    feature_count = local_weight.shape[0]
    columns = local_weight.shape[1]
    features = lax.dynamic_slice_in_dim(
        audio_hidden, feature_group * feature_count, feature_count, 1
    )
    rows = features
    partial_sum = jnp.dot(rows, local_weight, preferred_element_type=jnp.float32)
    padded = jnp.zeros((audio_rows, quarters * columns), jnp.float32)
    total = sum_by_parts(
        lax.dynamic_update_slice_in_dim(padded, partial_sum, quarter * columns, 1),
        (("seq_0", "seq_1", "seq_2"), "seq_3"),
    )
    audio_qkv = total.astype(jnp.bfloat16)
    audio_qkv = audio_qkv.reshape(audio_rows, 3, heads, HD)
    audio_q = audio_qkv[:, 0]
    audio_k = audio_qkv[:, 1]
    audio_v = audio_qkv[:, 2]
    query_blocks = video_query.reshape(blocks, block, heads, HD)
    key_blocks = video_kv[0].reshape(blocks, block, heads, HD)
    value_blocks = video_kv[1].reshape(blocks, block, heads, HD)
    clip_blocks = video_clip.reshape(blocks, block)

    def video_block(inputs):
        query, clips = inputs
        same = (clips[:, None] == audio_clip[None, :])[None]
        scores = (
            jnp.einsum("bhd,khd->hbk", query, audio_k, preferred_element_type=jnp.float32) * 0.125
        )
        scores = jnp.where(same, scores, NEG)
        top = jnp.max(scores, axis=2, keepdims=True)
        expo = jnp.exp(scores - top)
        probs = (expo / jnp.sum(expo, axis=2, keepdims=True)).astype(jnp.bfloat16)
        result = jnp.einsum("hbk,khd->bhd", probs, audio_v, preferred_element_type=jnp.float32)
        return result.reshape(block, width).astype(jnp.bfloat16)

    video_attn = lax.map(video_block, (query_blocks, clip_blocks)).reshape(local_rows, width)

    def audio_block(state, inputs):
        top, total, numer = state
        key, value, clips = inputs
        same = (audio_clip[:, None] == clips[None, :])[:, None, :]
        scores = (
            jnp.einsum("ahd,bhd->ahb", audio_q, key, preferred_element_type=jnp.float32) * 0.125
        )
        scores = jnp.where(same, scores, NEG)
        new_top = jnp.maximum(top, jnp.max(scores, axis=2))
        weights = jnp.where(same, jnp.exp(scores - new_top[:, :, None]), jnp.float32(0.0))
        factor = jnp.exp(top - new_top)
        total = total * factor + jnp.sum(weights, axis=2)
        added = jnp.einsum(
            "ahb,bhd->ahd", weights.astype(jnp.bfloat16), value, preferred_element_type=jnp.float32
        )
        numer = numer.reshape(audio_rows, heads, HD) * factor[:, :, None] + added
        return ((new_top, total, numer.reshape(audio_rows, width)), None)

    start_state = (
        jnp.full((audio_rows, heads), NEG, jnp.float32),
        jnp.zeros((audio_rows, heads), jnp.float32),
        jnp.zeros((audio_rows, width), jnp.float32),
    )
    (top, total, numer), unused = lax.scan(
        audio_block, start_state, (key_blocks, value_blocks, clip_blocks)
    )
    global_top = of_everyone(top, SEQ)
    factor = jnp.exp(top - global_top)
    scaled = (numer.reshape(audio_rows, heads, HD) * factor[:, :, None]).reshape(audio_rows, width)
    numer_rows, total_rows = sent_together(
        (scaled, total * factor), (("seq_0", "seq_1", "seq_2"), "seq_3"), 0, 1
    )
    share_rows = numer_rows.shape[0]
    finished = (numer_rows.reshape(share_rows, heads, HD) / total_rows[:, :, None]).reshape(
        share_rows, width
    )
    audio_attn = gathered_copies(finished.astype(jnp.bfloat16), SEQ, 0)
    rows = audio_attn
    audio_out = summed_on_arrival(
        jnp.dot(rows, audio_out_weight, preferred_element_type=jnp.float32), "head", 0
    )
    return (video_attn, audio_out.astype(jnp.bfloat16))


def solution(mesh):
    finer = Mesh(
        mesh.devices.reshape(2, 4, 4, 2, mesh.shape["head"]),
        ("seq_0", "seq_1", "seq_2", "seq_3", "head"),
    )
    placed = (
        P(SEQ, "head"),
        P(None, SEQ, "head"),
        P(SEQ),
        P(),
        P(SEQ, None, "head"),
        P(),
        P("head", SEQ),
    )
    return jax.shard_map(
        shards,
        mesh=finer,
        in_specs=placed,
        out_specs=(P(SEQ, "head"), P("head", SEQ)),
        check_vma=False,
    )
```

profile of v0, /device:TPU:0, one launch (start us, length us, event | category | flops | bytes accessed | tf_op | source)
XLA Modules:
  0.0 303.3 jit_solution(14467965716856249651)
XLA Ops:
  0.7 2.0 broadcast_in_dim.65
  2.7 2.1 convolution_dynamic-update-slice_fusion
  4.8 4.8 %reshape_reshape.2 = f32[32,2,4,3072]{3,2,1,0:T(4,128)} reshape(f32[256,3072]{1,0:T(8,128)} %convolution_dynamic-update-slice_fusion) | data formatting | bytes 6291456 | tf_op jit(solution)/shard_map/reshape;reshape | solution.py:18
  9.6 2.1 copy.81
  11.7 7.2 %all_to_all.45 = f32[2,32,4,3072]{3,2,1,0:T(4,128)} all-to-all(f32[2,32,4,3072]{3,2,1,0:T(4,128)S(1)} %copy.81), channel_id=1, replica_groups=mesh['seq_0'=2,'seq_1'=4,'seq_2'=4,'seq_3'=2,'head'=2] {'seq_3'}, dimensions={0} | all-to-all | bytes 6291456 | tf_op jit(solution)/shard_map/all_to_all | solution.py:23
  18.9 4.4 %reduce_sum.63 = f32[32,4,3072]{2,1,0:T(4,128)} reduce(f32[2,32,4,3072]{3,2,1,0:T(4,128)} %all_to_all.45, f32[]{:T(128)} %constant.84.clone.1), dimensions={0}, to_apply=%region_0.1 | reduce | flops 393216 | bytes 4718596 | tf_op jit(solution)/shard_map/reduce_sum | solution.py:24
  23.4 9.3 %all-to-all-start.1 = ((f32[32,4,3072]{2,1,0:T(4,128)}), f32[32,4,3072]{2,1,0:T(4,128)S(1)}, u32[]{:S(2)}, u32[]{:S(2)}) async-start(f32[32,4,3072]{2,1,0:T(4,128)} %reduce_sum.63), calls=%async_computation.1 | async-start | bytes 3145728 | tf_op jit(solution)/shard_map/all_to_all | solution.py:31
  32.7 22.9 %all-to-all-done.1 = f32[32,4,3072]{2,1,0:T(4,128)S(1)} async-done(((f32[32,4,3072]{2,1,0:T(4,128)}), f32[32,4,3072]{2,1,0:T(4,128)S(1)}, u32[]{:S(2)}, u32[]{:S(2)}) %all-to-all-start.1) | async-done | bytes 1572896 | tf_op jit(solution)/shard_map/all_to_all | solution.py:31
  55.8 1.1 broadcast_in_dim.66
  57.0 4.7 %all-to-all-start.2 = ((bf16[32,4,3072]{2,1,0:T(4,128)(2,1)}), bf16[32,4,3072]{2,1,0:T(4,128)(2,1)S(1)}, u32[]{:S(2)}, u32[]{:S(2)}) async-start(bf16[32,4,3072]{2,1,0:T(4,128)(2,1)} %broadcast_in_dim.66), calls=%async_computation.2 | async-start | bytes 1572864 | tf_op jit(solution)/shard_map/all_to_all | solution.py:44
  61.7 6.0 %fusion.44 = (bf16[1,2048,1024]{2,1,0:T(8,128)(2,1)}, bf16[1,2048,1024]{2,1,0:T(8,128)(2,1)}) fusion(bf16[2,2048,1024]{2,1,0:T(8,128)(2,1)} %param.12), kind=kLoop, calls=%fused_computation.61 | loop fusion | bytes 16777216 | tf_op jit(solution)/shard_map/slice | solution.py:118
  67.7 11.6 %reshape.117 = bf16[4,512,16,64]{3,2,1,0:T(8,128)(2,1)} reshape(bf16[1,2048,1024]{2,1,0:T(8,128)(2,1)} %get-tuple-element.243) | data formatting | bytes 8388608 | tf_op jit(solution)/shard_map/reshape;squeeze | solution.py:117
  79.3 9.8 %copy.90 = bf16[4,512,16,64]{1,3,2,0:T(8,128)(2,1)} copy(bf16[4,512,16,64]{3,2,1,0:T(8,128)(2,1)} %reshape.117) | data formatting | bytes 8388608
  89.0 11.6 %reshape.118 = bf16[4,512,16,64]{3,2,1,0:T(8,128)(2,1)} reshape(bf16[1,2048,1024]{2,1,0:T(8,128)(2,1)} %get-tuple-element.242) | data formatting | bytes 8388608 | tf_op jit(solution)/shard_map/reshape;squeeze | solution.py:118
  100.6 9.8 %copy.92 = bf16[4,512,16,64]{1,3,2,0:T(8,128)(2,1)} copy(bf16[4,512,16,64]{3,2,1,0:T(8,128)(2,1)} %reshape.118) | data formatting | bytes 8388608
  110.8 5.0 %all_to_all.46 = bf16[2,32,4,3072]{3,2,1,0:T(4,128)(2,1)S(1)} all-to-all(bf16[2,32,4,3072]{3,2,1,0:T(4,128)(2,1)S(1)} %broadcast_in_dim.67), channel_id=1, replica_groups=mesh['seq_0'=2,'seq_1'=4,'seq_2'=4,'seq_3'=2,'head'=2] {'seq_3'}, dimensions={0} | all-to-all | bytes 3145728 | tf_op jit(solution)/shard_map/all_to_all | solution.py:44
  116.6 3.3 %convert_element_type.40 = bf16[256,3,16,64]{3,2,1,0:T(8,128)(2,1)} reshape(bf16[32,2,4,3072]{3,2,1,0:T(4,128)(2,1)S(1)} %copy.83) | data formatting | bytes 3145728 | tf_op jit(solution)/shard_map/convert_element_type | solution.py:111
  119.9 3.8 %slice_bitcast_fusion = (bf16[256,16,64]{2,1,0:T(8,128)(2,1)S(1)}, bf16[256,16,64]{2,1,0:T(8,128)(2,1)}, bf16[256,16,64]{2,1,0:T(8,128)(2,1)}) fusion(bf16[256,3,16,64]{3,2,1,0:T(8,128)(2,1)} %convert_element_type.40), kind=kLoop, calls=%fused_computation.47 | loop fusion | bytes 3145728 | tf_op jit(solution)/shard_map/squeeze | solution.py:113
  123.7 0.8 copy.91
  124.7 61.6 %while.26 = (s32[]{:T(128)}, f32[256,16]{0,1:T(8,128)S(1)}, f32[256,16]{0,1:T(8,128)S(1)}, f32[256,1024]{0,1:T(8,128)S(1)}, s32[256]{0:T(256)S(1)}, /*index=5*/s...) while((s32[]{:T(128)}, f32[256,16]{0,1:T(8,128)S(1)}, ...), condition=%wide.region_9.10_spmd.clone, body=%wide.region_6.9_spmd.clone.sunk | while | flops 564809728 | bytes 64233624 | solution.py:159
  124.8 5.9 %fusion.71 = (f32[256,16]{0,1:T(8,128)S(1)}, f32[16,512,256]{2,1,0:T(8,128)}) fusion(pred[256,512]{0,1:T(8,128)(4,1)S(1)} %broadcast_compare_fusion.5, bf16[256,16,64]{0,2,1:T(8,128)(2,1)S(1)} %get-tuple-element.410, bf16[4,512,16,64]{1,3,2,0:T(8,128)(2,1)} %get-tuple-element.409, s32[]{:T(128)} %get-tuple-element.392), kind=kOutput, calls=%fused_computation.21.clone.1 | convolution fusion | flops 274722816 | bytes 10109440 | tf_op jit(solution)/shard_map/while/body/eval_jaxpr/ahd,bhd->ahb/dot_general | solution.py:141
  130.8 4.6 %fusion.72 = f32[256,16]{0,1:T(8,128)S(1)} fusion(f32[16,512,256]{2,1,0:T(8,128)} %get-tuple-element.354, f32[256,16]{0,1:T(8,128)S(1)} %select_maximum_fusion.2, pred[256,512]{0,1:T(8,128)(4,1)S(1)} %broadcast_compare_fusion.5), kind=kLoop, calls=%fused_computation.23.clone.1 | loop fusion | flops 10481664 | bytes 8552448 | tf_op jit(solution)/shard_map/while/body/eval_jaxpr/reduce_sum | solution.py:147
  135.4 1.2 copy-done.2
  136.6 3.5 %fusion.74 = f32[256,16,64]{0,2,1:T(8,128)S(1)} fusion(f32[16,512,256]{2,1,0:T(8,128)S(1)} %copy-done.2, f32[256,16]{0,1:T(8,128)S(1)} %select_maximum_fusion.2, pred[256,512]{0,1:T(8,128)(4,1)S(1)} %broadcast_compare_fusion.5, bf16[4,512,16,64]{1,3,2,0:T(8,128)(2,1)} %get-tuple-element.411, s32[]{:T(128)} %get-tuple-element.392, ...), kind=kOutput, calls=%fused_computation.27.clone.1 | convolution fusion | flops 279445504 | bytes 11698688 | tf_op jit(solution)/shard_map/while/body/eval_jaxpr/ahb,bhd->ahd/dot_general | solution.py:148
  140.2 5.9 %fusion.71 = (f32[256,16]{0,1:T(8,128)S(1)}, f32[16,512,256]{2,1,0:T(8,128)}) fusion(pred[256,512]{0,1:T(8,128)(4,1)S(1)} %broadcast_compare_fusion.5, bf16[256,16,64]{0,2,1:T(8,128)(2,1)S(1)} %get-tuple-element.410, bf16[4,512,16,64]{1,3,2,0:T(8,128)(2,1)} %get-tuple-element.409, s32[]{:T(128)} %get-tuple-element.392), kind=kOutput, calls=%fused_computation.21.clone.1 | convolution fusion | flops 274722816 | bytes 10109440 | tf_op jit(solution)/shard_map/while/body/eval_jaxpr/ahd,bhd->ahb/dot_general | solution.py:141
  146.2 4.6 %fusion.72 = f32[256,16]{0,1:T(8,128)S(1)} fusion(f32[16,512,256]{2,1,0:T(8,128)} %get-tuple-element.354, f32[256,16]{0,1:T(8,128)S(1)} %select_maximum_fusion.2, pred[256,512]{0,1:T(8,128)(4,1)S(1)} %broadcast_compare_fusion.5), kind=kLoop, calls=%fused_computation.23.clone.1 | loop fusion | flops 10481664 | bytes 8552448 | tf_op jit(solution)/shard_map/while/body/eval_jaxpr/reduce_sum | solution.py:147
  150.8 1.2 copy-done.2
  152.0 3.5 %fusion.74 = f32[256,16,64]{0,2,1:T(8,128)S(1)} fusion(f32[16,512,256]{2,1,0:T(8,128)S(1)} %copy-done.2, f32[256,16]{0,1:T(8,128)S(1)} %select_maximum_fusion.2, pred[256,512]{0,1:T(8,128)(4,1)S(1)} %broadcast_compare_fusion.5, bf16[4,512,16,64]{1,3,2,0:T(8,128)(2,1)} %get-tuple-element.411, s32[]{:T(128)} %get-tuple-element.392, ...), kind=kOutput, calls=%fused_computation.27.clone.1 | convolution fusion | flops 279445504 | bytes 11698688 | tf_op jit(solution)/shard_map/while/body/eval_jaxpr/ahb,bhd->ahd/dot_general | solution.py:148
  155.6 5.9 %fusion.71 = (f32[256,16]{0,1:T(8,128)S(1)}, f32[16,512,256]{2,1,0:T(8,128)}) fusion(pred[256,512]{0,1:T(8,128)(4,1)S(1)} %broadcast_compare_fusion.5, bf16[256,16,64]{0,2,1:T(8,128)(2,1)S(1)} %get-tuple-element.410, bf16[4,512,16,64]{1,3,2,0:T(8,128)(2,1)} %get-tuple-element.409, s32[]{:T(128)} %get-tuple-element.392), kind=kOutput, calls=%fused_computation.21.clone.1 | convolution fusion | flops 274722816 | bytes 10109440 | tf_op jit(solution)/shard_map/while/body/eval_jaxpr/ahd,bhd->ahb/dot_general | solution.py:141
  161.6 4.6 %fusion.72 = f32[256,16]{0,1:T(8,128)S(1)} fusion(f32[16,512,256]{2,1,0:T(8,128)} %get-tuple-element.354, f32[256,16]{0,1:T(8,128)S(1)} %select_maximum_fusion.2, pred[256,512]{0,1:T(8,128)(4,1)S(1)} %broadcast_compare_fusion.5), kind=kLoop, calls=%fused_computation.23.clone.1 | loop fusion | flops 10481664 | bytes 8552448 | tf_op jit(solution)/shard_map/while/body/eval_jaxpr/reduce_sum | solution.py:147
  166.2 1.2 copy-done.2
  167.4 3.5 %fusion.74 = f32[256,16,64]{0,2,1:T(8,128)S(1)} fusion(f32[16,512,256]{2,1,0:T(8,128)S(1)} %copy-done.2, f32[256,16]{0,1:T(8,128)S(1)} %select_maximum_fusion.2, pred[256,512]{0,1:T(8,128)(4,1)S(1)} %broadcast_compare_fusion.5, bf16[4,512,16,64]{1,3,2,0:T(8,128)(2,1)} %get-tuple-element.411, s32[]{:T(128)} %get-tuple-element.392, ...), kind=kOutput, calls=%fused_computation.27.clone.1 | convolution fusion | flops 279445504 | bytes 11698688 | tf_op jit(solution)/shard_map/while/body/eval_jaxpr/ahb,bhd->ahd/dot_general | solution.py:148
  171.0 5.9 %fusion.71 = (f32[256,16]{0,1:T(8,128)S(1)}, f32[16,512,256]{2,1,0:T(8,128)}) fusion(pred[256,512]{0,1:T(8,128)(4,1)S(1)} %broadcast_compare_fusion.5, bf16[256,16,64]{0,2,1:T(8,128)(2,1)S(1)} %get-tuple-element.410, bf16[4,512,16,64]{1,3,2,0:T(8,128)(2,1)} %get-tuple-element.409, s32[]{:T(128)} %get-tuple-element.392), kind=kOutput, calls=%fused_computation.21.clone.1 | convolution fusion | flops 274722816 | bytes 10109440 | tf_op jit(solution)/shard_map/while/body/eval_jaxpr/ahd,bhd->ahb/dot_general | solution.py:141
  177.0 4.6 %fusion.72 = f32[256,16]{0,1:T(8,128)S(1)} fusion(f32[16,512,256]{2,1,0:T(8,128)} %get-tuple-element.354, f32[256,16]{0,1:T(8,128)S(1)} %select_maximum_fusion.2, pred[256,512]{0,1:T(8,128)(4,1)S(1)} %broadcast_compare_fusion.5), kind=kLoop, calls=%fused_computation.23.clone.1 | loop fusion | flops 10481664 | bytes 8552448 | tf_op jit(solution)/shard_map/while/body/eval_jaxpr/reduce_sum | solution.py:147
  181.6 1.2 copy-done.2
  182.8 3.5 %fusion.74 = f32[256,16,64]{0,2,1:T(8,128)S(1)} fusion(f32[16,512,256]{2,1,0:T(8,128)S(1)} %copy-done.2, f32[256,16]{0,1:T(8,128)S(1)} %select_maximum_fusion.2, pred[256,512]{0,1:T(8,128)(4,1)S(1)} %broadcast_compare_fusion.5, bf16[4,512,16,64]{1,3,2,0:T(8,128)(2,1)} %get-tuple-element.411, s32[]{:T(128)} %get-tuple-element.392, ...), kind=kOutput, calls=%fused_computation.27.clone.1 | convolution fusion | flops 279445504 | bytes 11698688 | tf_op jit(solution)/shard_map/while/body/eval_jaxpr/ahb,bhd->ahd/dot_general | solution.py:148
  186.4 25.6 %all_to_all.47 = f32[64,256,16]{1,2,0:T(8,128)S(1)} all-to-all(f32[64,256,16]{1,2,0:T(8,128)S(1)} %broadcast_in_dim.94), channel_id=1, replica_groups=mesh['seq_0'=2,'seq_1'=4,'seq_2'=4,'seq_3'=2,'head'=2] {'seq_0','seq_1',..., dimensions={0} | all-to-all | bytes 2097152 | tf_op jit(solution)/shard_map/all_to_all | solution.py:44
  213.4 4.7 %all_to_all.48 = f32[2,32,4,1040]{3,2,1,0:T(4,128)S(1)} all-to-all(f32[2,32,4,1040]{3,2,1,0:T(4,128)S(1)} %copy.95), channel_id=1, replica_groups=mesh['seq_0'=2,'seq_1'=4,'seq_2'=4,'seq_3'=2,'head'=2] {'seq_3'}, dimensions={0} | all-to-all | bytes 2129920 | tf_op jit(solution)/shard_map/all_to_all | solution.py:23
  218.6 17.1 %all_to_all.49 = f32[32,4,1040]{2,1,0:T(4,128)S(1)} all-to-all(f32[32,4,1040]{2,1,0:T(4,128)S(1)} %reduce_sum.65), channel_id=1, replica_groups=mesh['seq_0'=2,'seq_1'=4,'seq_2'=4,'seq_3'=2,'head'=2] {'seq_0','seq_1',..., dimensions={0} | all-to-all | bytes 1064960 | tf_op jit(solution)/shard_map/all_to_all | solution.py:31
  235.9 1.0 broadcast_in_dim.95
  236.9 4.9 %all-to-all-start.7 = ((bf16[64,4,1024]{2,1,0:T(4,128)(2,1)}), bf16[64,4,1024]{2,1,0:T(4,128)(2,1)S(1)}, u32[]{:S(2)}, u32[]{:S(2)}) async-start(bf16[64,4,1024]{2,1,0:T(4,128)(2,1)} %broadcast_in_dim.95), calls=%async_computation.7 | async-start | bytes 1048576 | tf_op jit(solution)/shard_map/all_to_all | solution.py:44
  241.8 11.6 %reshape.116 = bf16[4,512,16,64]{3,2,1,0:T(8,128)(2,1)} reshape(bf16[2048,1024]{1,0:T(8,128)(2,1)} %param.11) | data formatting | bytes 8388608 | tf_op jit(solution)/shard_map/reshape | solution.py:116
  253.4 9.9 %copy.84 = bf16[4,512,16,64]{1,3,2,0:T(8,128)(2,1)} copy(bf16[4,512,16,64]{3,2,1,0:T(8,128)(2,1)} %reshape.116) | data formatting | bytes 8388608 | tf_op jit(solution)/shard_map/while | solution.py:134
  263.3 0.8 copy.85
  264.1 1.7 copy.86
  265.9 0.9 fusion.37
  266.8 4.0 %all-to-all-start.8 = ((f32[2,128,32]{1,2,0:T(8,128)}), f32[2,128,32]{1,2,0:T(8,128)S(1)}, u32[]{:S(2)}, u32[]{:S(2)}) async-start(f32[2,128,32]{1,2,0:T(8,128)} %fusion.37), calls=%async_computation.8 | async-start | bytes 65536 | tf_op jit(solution)/shard_map/all_to_all | solution.py:23
  270.8 31.2 %while.25 = (s32[]{:T(128)}, bf16[4,512,1024]{2,1,0:T(8,128)(2,1)}, s32[4,512]{1,0:T(4,128)S(1)}, s32[256]{0:T(256)S(1)}, bf16[4,512,16,64]{1,3,2,0:T(8,128)(2,1...) while((s32[]{:T(128)}, bf16[4,512,1024]{2,1,0:T(8,128)(2,1)}, ...), condition=%wide.region_5.6_spmd, body=%wide.region_2.5_spmd.sunk | while | flops 554303744 | bytes 43327604 | solution.py:134
  270.8 2.5 fusion.65
  273.5 2.6 fusion.66
  276.1 0.9 fusion.67
  277.6 1.0 constant_dynamic-update-slice_fusion.2
  278.6 2.5 fusion.65
  281.3 2.6 fusion.66
  283.9 0.9 fusion.67
  285.4 1.0 constant_dynamic-update-slice_fusion.2
  286.4 2.5 fusion.65
  289.1 2.6 fusion.66
  291.8 0.9 fusion.67
  293.2 1.0 constant_dynamic-update-slice_fusion.2
  294.2 2.5 fusion.65
  296.9 2.6 fusion.66
  299.6 0.9 fusion.67
  301.0 1.0 constant_dynamic-update-slice_fusion.2
  (86 shorter events, 8.6 us)
Async XLA Ops:
  0.6 2.1 copy-start
  23.4 32.2 %all-to-all-start.1 = ((f32[32,4,3072]{2,1,0:T(4,128)}), f32[32,4,3072]{2,1,0:T(4,128)S(1)}, u32[]{:S(2)}, u32[]{:S(2)}) async-start(f32[32,4,3072]{2,1,0:T(4,128)} %reduce_sum.63), calls=%async_computation.1 | async-start | bytes 3145728 | tf_op jit(solution)/shard_map/all_to_all | solution.py:31
  57.0 53.4 %all-to-all-start.2 = ((bf16[32,4,3072]{2,1,0:T(4,128)(2,1)}), bf16[32,4,3072]{2,1,0:T(4,128)(2,1)S(1)}, u32[]{:S(2)}, u32[]{:S(2)}) async-start(bf16[32,4,3072]{2,1,0:T(4,128)(2,1)} %broadcast_in_dim.66), calls=%async_computation.2 | async-start | bytes 1572864 | tf_op jit(solution)/shard_map/all_to_all | solution.py:44
  100.6 9.8 %copy-start.8 = (s32[2048]{0:T(1024)S(1)}, s32[2048]{0:T(1024)}, u32[]{:S(2)}) copy-start(s32[2048]{0:T(1024)} %param.13) | copy-start | bytes 24580
  115.8 8.9 %copy-start.6 = (s32[256]{0:T(256)S(1)}, s32[256]{0:T(256)}, u32[]{:S(2)}) copy-start(s32[256]{0:T(256)} %param.16) | copy-start | bytes 3076
  130.8 5.8 %copy-start.2 = (f32[16,512,256]{2,1,0:T(8,128)S(1)}, f32[16,512,256]{2,1,0:T(8,128)}, u32[]{:S(2)}) copy-start(f32[16,512,256]{2,1,0:T(8,128)} %get-tuple-element.354) | copy-start | bytes 25165828 | tf_op jit(solution)/shard_map/while
  146.2 5.8 %copy-start.2 = (f32[16,512,256]{2,1,0:T(8,128)S(1)}, f32[16,512,256]{2,1,0:T(8,128)}, u32[]{:S(2)}) copy-start(f32[16,512,256]{2,1,0:T(8,128)} %get-tuple-element.354) | copy-start | bytes 25165828 | tf_op jit(solution)/shard_map/while
  161.6 5.8 %copy-start.2 = (f32[16,512,256]{2,1,0:T(8,128)S(1)}, f32[16,512,256]{2,1,0:T(8,128)}, u32[]{:S(2)}) copy-start(f32[16,512,256]{2,1,0:T(8,128)} %get-tuple-element.354) | copy-start | bytes 25165828 | tf_op jit(solution)/shard_map/while
  177.0 5.8 %copy-start.2 = (f32[16,512,256]{2,1,0:T(8,128)S(1)}, f32[16,512,256]{2,1,0:T(8,128)}, u32[]{:S(2)}) copy-start(f32[16,512,256]{2,1,0:T(8,128)} %get-tuple-element.354) | copy-start | bytes 25165828 | tf_op jit(solution)/shard_map/while
  236.9 28.9 %all-to-all-start.7 = ((bf16[64,4,1024]{2,1,0:T(4,128)(2,1)}), bf16[64,4,1024]{2,1,0:T(4,128)(2,1)S(1)}, u32[]{:S(2)}, u32[]{:S(2)}) async-start(bf16[64,4,1024]{2,1,0:T(4,128)(2,1)} %broadcast_in_dim.95), calls=%async_computation.7 | async-start | bytes 1048576 | tf_op jit(solution)/shard_map/all_to_all | solution.py:44
  253.3 9.9 %copy-start.4 = (bf16[256,16,64]{2,1,0:T(8,128)(2,1)S(1)}, bf16[256,16,64]{2,1,0:T(8,128)(2,1)}, u32[]{:S(2)}) copy-start(bf16[256,16,64]{2,1,0:T(8,128)(2,1)} %get-tuple-element.246) | copy-start | bytes 1572868
  253.3 10.8 %copy-start.3 = (bf16[256,16,64]{2,1,0:T(8,128)(2,1)S(1)}, bf16[256,16,64]{2,1,0:T(8,128)(2,1)}, u32[]{:S(2)}) copy-start(bf16[256,16,64]{2,1,0:T(8,128)(2,1)} %get-tuple-element.245) | copy-start | bytes 1572868
  253.4 12.6 %copy-start.7 = (bf16[1024,32]{0,1:T(8,128)(2,1)S(1)}, bf16[1024,32]{0,1:T(8,128)(2,1)}, u32[]{:S(2)}) copy-start(bf16[1024,32]{0,1:T(8,128)(2,1)} %param.17) | copy-start | bytes 196612
  266.8 35.2 %all-to-all-start.8 = ((f32[2,128,32]{1,2,0:T(8,128)}), f32[2,128,32]{1,2,0:T(8,128)S(1)}, u32[]{:S(2)}, u32[]{:S(2)}) async-start(f32[2,128,32]{1,2,0:T(8,128)} %fusion.37), calls=%async_computation.8 | async-start | bytes 65536 | tf_op jit(solution)/shard_map/all_to_all | solution.py:23
  273.5 2.6 copy-start.5
  281.3 2.6 copy-start.5
  289.1 2.6 copy-start.5
  296.9 2.6 copy-start.5
  302.0 1.2 copy-start.1
where the time goes:
time: 307 us; the launch traced here: 303 us
  local copies, waits for them, and re-layouts  106 us (35%)
  blocking collectives  59.6 us (19%)
  matrix products  54 us (18%)
  other arithmetic  36.4 us (12%)
  starting transfers between devices  22.9 us (7%)
  waiting for transfers between devices  22.9 us (7%)
    all_to_all x2, blocking collectives, copy_for_each(): lax.all_to_all(jnp.broadcast_to(x[None], (devices, *x.shape)), axis, 0, 0...  30.6 us
    dot_general x4, matrix products, audio_block(): jnp.einsum('ahd,bhd->ahb', audio_q, key, preferred_element_type=jnp.float32)  23.6 us
    all_to_all x1, waiting for transfers between devices, summed_rows(): lax.all_to_all(nearer, far, split_axis=0, concat_axis=0, tiled=True)  22.9 us
    unnamed x17, local copies, waits for them, and re-layouts  21 us
    reduce_sum x4, other arithmetic, audio_block(): total = total * factor + jnp.sum(weights, axis=2)  18.4 us
    all_to_all x1, blocking collectives, summed_rows(): lax.all_to_all(nearer, far, split_axis=0, concat_axis=0, tiled=True)  17.1 us
    dot_general x4, matrix products, audio_block(): jnp.einsum('ahb,bhd->ahd', weights.astype(jnp.bfloat16), value, preferred...  13.8 us
    while x3, local copies, waits for them, and re-layouts, shards(): lax.map(video_block, (query_blocks, clip_blocks)).reshape(local_rows, width)  12.4 us
  transfers between devices with their start and end apart: 4, of which 1 were waited for; matrix products, arithmetic and copies ran while one was open for 34% of the time, Pallas kernels for 0%

commit v1 on v0

v1 whole, which is shorter than its diff:
```python
import functools

import jax
import jax.numpy as jnp
from jax import lax
from jax.experimental import pallas as pl
from jax.experimental.pallas import tpu as pltpu
from jax.sharding import PartitionSpec as P

F32 = jnp.float32
BF = jnp.bfloat16
NT = (((1,), (1,)), ((), ()))
BIG = -1e30
MESH = pl.DeviceIdType.MESH
VMEM = pl.BlockSpec(memory_space=pltpu.VMEM)
ANY = pl.BlockSpec(memory_space=pl.ANY)
CHIPS = 32
GROUP = 8


def place():
    seq = lax.axis_index("seq")
    head = lax.axis_index("head")
    return seq // 2, seq % 2, head


def remote(src, dst, send, recv, chip, core, head):
    return pltpu.make_async_remote_copy(
        src_ref=src,
        dst_ref=dst,
        send_sem=send,
        recv_sem=recv,
        device_id=(chip * 2 + core, head),
        device_id_type=MESH,
    )


def greet(chip, core, head, with_head):
    barrier = pltpu.get_barrier_semaphore()

    def one(i, _):
        to = lax.rem(chip + i, CHIPS)
        pl.semaphore_signal(barrier, inc=1, device_id=(to * 2 + core, head), device_id_type=MESH)
        return 0

    lax.fori_loop(1, CHIPS, one, 0)
    pl.semaphore_signal(
        barrier, inc=1, device_id=(chip * 2 + 1 - core, head), device_id_type=MESH
    )
    count = CHIPS
    if with_head:
        pl.semaphore_signal(
            barrier, inc=1, device_id=(chip * 2 + core, 1 - head), device_id_type=MESH
        )
        count += 1
    pl.semaphore_wait(barrier, count)


def spread(groups, send_sem, recv_sem, pass_send, pass_recv, chip, core, head, slot):
    own = slot(chip, core)

    def send(i):
        to = lax.rem(chip + i, CHIPS)
        return remote(own, own, send_sem.at[i], recv_sem.at[i], to, core, head)

    def start(i, _):
        send(i).start()
        return 0

    def hand_on(i):
        frm = lax.rem(chip + CHIPS - i, CHIPS)
        block = slot(frm, core)
        return remote(block, block, pass_send.at[i], pass_recv.at[i], chip, 1 - core, head)

    def handed(i):
        frm = lax.rem(chip + CHIPS - i, CHIPS)
        block = slot(frm, 1 - core)
        return remote(block, block, pass_send.at[i], pass_recv.at[i], chip, 1 - core, head)

    def begin():
        hand_on(0).start()
        lax.fori_loop(1, CHIPS, start, 0)

    def relay(i, _):
        frm = lax.rem(chip + CHIPS - i, CHIPS)
        block = slot(frm, core)
        remote(block, block, send_sem.at[i], recv_sem.at[i], frm, core, head).wait_recv()
        hand_on(i).start()
        return 0

    def middle():
        lax.fori_loop(1, CHIPS, relay, 0)

    def finish():
        def arrived(i, _):
            handed(i).wait_recv()
            hand_on(i).wait_send()
            return 0

        def sent(i, _):
            send(i).wait_send()
            return 0

        lax.fori_loop(0, CHIPS, arrived, 0)
        lax.fori_loop(1, CHIPS, sent, 0)

    return begin, middle, finish


def project_kernel(x, w, out, xs, part, near, total, far, sem, s2, r2, s3, r3, s4, r4):
    chip, core, head = place()
    quarter, g = chip // GROUP, chip % GROUP
    fg = g * 2 + core
    load = pltpu.make_async_copy(
        x.at[:, pl.ds(pl.multiple_of(fg * 128, 128), 128)], xs, sem.at[0]
    )
    load.start()
    load.wait()
    part[...] = jnp.dot(xs[...], w[0], preferred_element_type=F32)
    greet(chip, core, head, False)
    theirs = part.at[pl.ds(pl.multiple_of((1 - core) * 128, 128), 128)]
    swap = remote(theirs, near, sem.at[1], sem.at[2], chip, 1 - core, head)
    swap.start()
    swap.wait_recv()
    total[...] = part[pl.ds(pl.multiple_of(core * 128, 128), 128), :] + near[...]

    def scatter(i):
        to = lax.rem(g + i, GROUP)
        rows = total.at[pl.ds(pl.multiple_of(to * 16, 16), 16)]
        return remote(rows, far.at[i], s2.at[i], r2.at[i], quarter * GROUP + to, core, head)

    for i in range(1, GROUP):
        scatter(i).start()
    acc = total[pl.ds(pl.multiple_of(g * 16, 16), 16), :]
    for i in range(1, GROUP):
        scatter(i).wait_recv()
        acc = acc + far[i]

    def slot(c, k):
        row = pl.multiple_of((k * GROUP + lax.rem(c, GROUP)) * 16, 16)
        return out.at[c // GROUP, pl.ds(row, 16)]

    slot(chip, core)[...] = acc.astype(BF)
    begin, middle, finish = spread(None, s3, r3, s4, r4, chip, core, head, slot)
    begin()
    middle()
    finish()
    for i in range(1, GROUP):
        scatter(i).wait_send()
    swap.wait_send()


def project(x, w):
    return pl.pallas_call(
        project_kernel,
        out_shape=jax.ShapeDtypeStruct((4, 256, 768), BF),
        in_specs=[ANY, VMEM],
        out_specs=VMEM,
        scratch_shapes=[
            pltpu.VMEM((256, 128), BF),
            pltpu.VMEM((256, 768), F32),
            pltpu.VMEM((128, 768), F32),
            pltpu.VMEM((128, 768), F32),
            pltpu.VMEM((GROUP, 16, 768), F32),
            pltpu.SemaphoreType.DMA((3,)),
            pltpu.SemaphoreType.DMA((GROUP,)),
            pltpu.SemaphoreType.DMA((GROUP,)),
            pltpu.SemaphoreType.DMA((CHIPS,)),
            pltpu.SemaphoreType.DMA((CHIPS,)),
            pltpu.SemaphoreType.DMA((CHIPS,)),
            pltpu.SemaphoreType.DMA((CHIPS,)),
        ],
        compiler_params=pltpu.CompilerParams(
            collective_id=0, has_side_effects=True, vmem_limit_bytes=16 * 2**20
        ),
    )(x, w)


def lanes(j):
    return pl.ds(pl.multiple_of(j * 128, 128), 128)


def columns(qkv, block):
    return qkv[block // 6, :, lanes(block % 6)]


def both_heads(x, mask):
    lane = lax.broadcasted_iota(jnp.int32, x.shape, 1)
    zero = jnp.zeros_like(x)
    x = (x.astype(F32) * 0.125).astype(BF)
    first = jnp.concatenate([jnp.where(lane < 64, x, zero), mask], 1)
    second = jnp.concatenate([jnp.where(lane >= 64, x, zero), mask], 1)
    return jnp.concatenate([first, second], 0)


def audio_kernel(qkv, mask, hot, kv, numer, stat, sa, sb, ma, mb):
    size = 512
    pieces = kv.shape[1] // size
    stat[...] = jnp.zeros_like(stat)
    lane = lax.broadcasted_iota(jnp.int32, (256, 128), 1)
    ones = jnp.ones((size, 128), BF)

    def query(j):
        return both_heads(columns(qkv, j), mask[...])

    def score(j, q2, c, s_ref, top):
        rows = pl.ds(c * size, size)
        keys = jnp.concatenate([kv[0, rows, lanes(j)], hot[rows, :]], 1)
        s = lax.dot_general(q2, keys, NT, preferred_element_type=F32)
        s_ref[:, c * size : (c + 1) * size] = s
        for t in range(size // 128):
            piece = s[:, t * 128 : (t + 1) * 128]
            top = piece if top is None else jnp.maximum(top, piece)
        return top

    def keep(top, m_ref):
        m_ref[...] = jnp.broadcast_to(jnp.max(top, axis=1, keepdims=True), (512, 128))

    def weigh(j, top, c, s_ref, acc):
        rows = pl.ds(c * size, size)
        wide = jnp.concatenate([top] * (size // 128), 1)
        weights = jnp.exp(s_ref[:, c * size : (c + 1) * size] - wide).astype(BF)
        values = jnp.concatenate([kv[1, rows, lanes(j)], ones], 1)
        r = jnp.dot(weights, values, preferred_element_type=F32)
        return r if acc is None else acc + r

    def step(j, following, s_ref, m_ref, s_next, m_next):
        q2 = query(following)
        top, acc, now = None, None, m_ref[...]
        for c in range(pieces):
            top = score(following, q2, c, s_next, top)
            acc = weigh(j, now, c, s_ref, acc)
        keep(top, m_next)
        numer[:, lanes(j)] = jnp.where(lane < 64, acc[:256, :128], acc[256:, :128])
        st = stat[...]
        st = jnp.where(lane == 2 * j, now[:256], st)
        st = jnp.where(lane == 2 * j + 1, now[256:], st)
        st = jnp.where(lane == 2 * j + 64, acc[:256, 128:], st)
        st = jnp.where(lane == 2 * j + 65, acc[256:, 128:], st)
        stat[...] = st

    q2, top = query(0), None
    for c in range(pieces):
        top = score(0, q2, c, sa, top)
    keep(top, ma)

    def two(i, _):
        step(2 * i, 2 * i + 1, sa, ma, sb, mb)
        step(2 * i + 1, jnp.minimum(2 * i + 2, 7), sb, mb, sa, ma)
        return 0

    lax.fori_loop(0, 4, two, 0)


def audio_part(qkv, mask, hot, kv):
    return pl.pallas_call(
        audio_kernel,
        out_shape=(
            jax.ShapeDtypeStruct((256, 1024), F32),
            jax.ShapeDtypeStruct((256, 128), F32),
        ),
        in_specs=[VMEM] * 4,
        out_specs=(VMEM, VMEM),
        scratch_shapes=[
            pltpu.VMEM((512, 2048), F32),
            pltpu.VMEM((512, 2048), F32),
            pltpu.VMEM((512, 128), F32),
            pltpu.VMEM((512, 128), F32),
        ],
        compiler_params=pltpu.CompilerParams(vmem_limit_bytes=40 * 2**20),
    )(qkv, mask, hot, kv)


def video_pair(j, qkv, mask, hot, vq, vout):
    size = 1024
    lane = lax.broadcasted_iota(jnp.int32, (size, 128), 1)
    k2 = both_heads(columns(qkv, j + 8), mask[...])
    values = jnp.concatenate([columns(qkv, j + 16), jnp.ones((256, 128), BF)], 1)
    for c in range(vq.shape[0] // size):
        rows = pl.ds(c * size, size)
        q = jnp.concatenate([vq[rows, lanes(j)], hot[rows, :]], 1)
        s = lax.dot_general(q, k2, NT, preferred_element_type=F32)
        r = []
        for h in range(2):
            sh = s[:, h * 256 : (h + 1) * 256]
            p = jnp.exp(sh - jnp.max(sh, axis=1, keepdims=True)).astype(BF)
            r.append(jnp.dot(p, values, preferred_element_type=F32))
        num = jnp.where(lane < 64, r[0][:, :128], r[1][:, :128])
        den = jnp.where(lane < 64, r[0][:, 128:], r[1][:, 128:])
        vout[rows, lanes(j)] = (num / den).astype(BF)


def video_kernel(qkv, mask, hot, vq, vout):
    def one(j, _):
        video_pair(j, qkv, mask, hot, vq, vout)
        return 0

    lax.fori_loop(0, 8, one, 0)


def video_part(qkv, mask, hot, vq):
    return pl.pallas_call(
        video_kernel,
        out_shape=jax.ShapeDtypeStruct(vq.shape, BF),
        in_specs=[VMEM] * 4,
        out_specs=VMEM,
        compiler_params=pltpu.CompilerParams(vmem_limit_bytes=40 * 2**20),
    )(qkv, mask, hot, vq)


def widened(f, first):
    n = f.shape[0]
    lane = lax.broadcasted_iota(jnp.int32, (n, 128), 1)
    out = []
    for p in range(4):
        a = jnp.broadcast_to(f[:, first + 2 * p : first + 2 * p + 1], (n, 128))
        b = jnp.broadcast_to(f[:, first + 2 * p + 1 : first + 2 * p + 2], (n, 128))
        out.append(jnp.where(lane < 64, a, b))
    return jnp.concatenate(out, 1)


def of_core(f, core, shift):
    return jnp.where(core == 0, f[:, shift : shift + 8], f[:, shift + 8 : shift + 16])


def finish_kernel(
    with_video, numer, stat, wout, qkv, mask, hot, vq, *refs
):
    if with_video:
        vout, refs = refs[0], refs[1:]
    out, rn, rs, comb, land, gath, mine, back, swap, sem, s2, r2, s3, r3, s4, r4 = refs
    chip, core, head = place()

    def video(j0, j1):
        if with_video:
            def one(j, _):
                video_pair(j, qkv, mask, hot, vq, vout)
                return 0

            lax.fori_loop(j0, j1, one, 0)

    greet(chip, core, head, True)
    send_n = remote(
        numer.at[:, pl.ds(pl.multiple_of((1 - core) * 512, 512), 512)],
        rn, sem.at[0], sem.at[1], chip, 1 - core, head,
    )
    send_s = remote(stat, rs, sem.at[2], sem.at[3], chip, 1 - core, head)
    send_n.start()
    send_s.start()
    video(0, 1)
    send_s.wait_recv()
    send_n.wait_recv()

    lane = lax.broadcasted_iota(jnp.int32, (256, 128), 1)
    a, b = stat[...], rs[...]
    top = jnp.maximum(a, b)
    fa = jnp.where(lane < 64, jnp.exp(a - top), 0.0)
    fb = jnp.where(lane < 64, jnp.exp(b - top), 0.0)
    den = a * pltpu.roll(fa, 64, 1) + b * pltpu.roll(fb, 64, 1)
    comb[:, 512:] = jnp.where(lane < 64, top, den)
    own = numer[:, pl.ds(pl.multiple_of(core * 512, 512), 512)]
    wa, wb = widened(of_core(fa, core, 0), 0), widened(of_core(fb, core, 0), 0)
    comb[:, :512] = own * wa + rn[...] * wb

    def scatter(i):
        to = lax.rem(chip + i, CHIPS)
        rows = comb.at[pl.ds(pl.multiple_of(to * 8, 8), 8)]
        return remote(rows, land.at[i], s2.at[i], r2.at[i], to, core, head)

    def start(i, _):
        scatter(i).start()
        return 0

    lax.fori_loop(1, CHIPS, start, 0)
    land[0] = comb[pl.ds(pl.multiple_of(chip * 8, 8), 8), :]
    video(1, 4)

    def landed(i, _):
        scatter(i).wait_recv()
        return 0

    lax.fori_loop(1, CHIPS, landed, 0)
    stats = [land[i, :, 512:] for i in range(CHIPS)]
    top = functools.reduce(jnp.maximum, stats)
    lane = lax.broadcasted_iota(jnp.int32, (8, 128), 1)
    total = jnp.zeros((8, 512), F32)
    den = jnp.zeros((8, 128), F32)
    for i in range(CHIPS):
        f = jnp.where(lane < 64, jnp.exp(stats[i] - top), 0.0)
        den = den + stats[i] * pltpu.roll(f, 64, 1)
        total = total + land[i, :, :512] * widened(of_core(f, core, 0), 0)
    attn = total / widened(of_core(den, core, 64), 0)

    def slot(c, k):
        return gath.at[k, c]

    slot(chip, core)[...] = jnp.concatenate([attn[:, :256], attn[:, 256:]], 0).astype(BF)
    begin, middle, end = spread(None, s3, r3, s4, r4, chip, core, head, slot)
    begin()
    video(4, 6)
    middle()
    video(6, 7)
    end()
    acc = None
    for k in range(2):
        rows = gath[k].reshape(CHIPS * 16, 256)
        for h in range(2):
            at = k * 512 + h * 256
            r = jnp.dot(rows, wout[at : at + 256, :], preferred_element_type=F32)
            r = r.reshape(CHIPS, 16, 32)[:, h * 8 : (h + 1) * 8]
            acc = r if acc is None else acc + r
    mine[...] = acc.reshape(256, 32)

    def folded(x):
        return jnp.concatenate([x[32 * t : 32 * t + 32] for t in range(4)], 1)

    swap[...] = folded(mine[pl.ds(pl.multiple_of((1 - head) * 128, 128), 128), :])
    across = remote(swap, back, sem.at[4], sem.at[5], chip, core, 1 - head)
    across.start()
    video(7, 8)
    across.wait_recv()
    half = folded(mine[pl.ds(pl.multiple_of(head * 128, 128), 128), :]) + back[...]
    for t in range(4):
        out[32 * t : 32 * t + 32, :] = half[:, 32 * t : 32 * t + 32].astype(BF)
    across.wait_send()
    send_n.wait_send()
    send_s.wait_send()

    def sent(i, _):
        scatter(i).wait_send()
        return 0

    lax.fori_loop(1, CHIPS, sent, 0)


def finish_part(numer, stat, wout, qkv, mask, hot, vq, with_video):
    shapes = [jax.ShapeDtypeStruct((128, 32), BF)]
    if with_video:
        shapes = [jax.ShapeDtypeStruct(vq.shape, BF)] + shapes
    return pl.pallas_call(
        functools.partial(finish_kernel, with_video),
        out_shape=tuple(shapes),
        in_specs=[VMEM] * 6 + [VMEM if with_video else ANY],
        out_specs=tuple([VMEM] * len(shapes)),
        scratch_shapes=[
            pltpu.VMEM((256, 512), F32),
            pltpu.VMEM((256, 128), F32),
            pltpu.VMEM((256, 640), F32),
            pltpu.VMEM((CHIPS, 8, 640), F32),
            pltpu.VMEM((2, CHIPS, 16, 256), BF),
            pltpu.VMEM((256, 32), F32),
            pltpu.VMEM((32, 128), F32),
            pltpu.VMEM((32, 128), F32),
            pltpu.SemaphoreType.DMA((6,)),
            pltpu.SemaphoreType.DMA((CHIPS,)),
            pltpu.SemaphoreType.DMA((CHIPS,)),
            pltpu.SemaphoreType.DMA((CHIPS,)),
            pltpu.SemaphoreType.DMA((CHIPS,)),
            pltpu.SemaphoreType.DMA((CHIPS,)),
            pltpu.SemaphoreType.DMA((CHIPS,)),
        ],
        compiler_params=pltpu.CompilerParams(
            collective_id=1, has_side_effects=True, vmem_limit_bytes=40 * 2**20
        ),
    )(numer, stat, wout, qkv, mask, hot, vq)


WITH_VIDEO = True


def shards(vq, kv, video_clip, x, w, audio_clip, wout):
    number = jnp.arange(128)
    hot = (video_clip[:, None] == number[None, :]).astype(BF)
    differs = (audio_clip[:, None] != number[None, :]) & (number[None, :] < 8)
    mask = jnp.where(differs, BIG, 0.0).astype(BF)
    qkv = project(x, w)
    numer, stat = audio_part(qkv, mask, hot, kv)
    if WITH_VIDEO:
        return finish_part(numer, stat, wout, qkv, mask, hot, vq, True)
    (audio_out,) = finish_part(numer, stat, wout, qkv, mask, hot, vq, False)
    return video_part(qkv, mask, hot, vq), audio_out


def solution(mesh):
    return jax.shard_map(
        shards,
        mesh=mesh,
        in_specs=(
            P("seq", "head"),
            P(None, "seq", "head"),
            P("seq"),
            P(),
            P("seq", None, "head"),
            P(),
            P("head", "seq"),
        ),
        out_specs=(P("seq", "head"), P("head", "seq")),
        check_vma=False,
    )
```

time: 307 us -> 97.4 us (0.32); the launches traced: 303 us -> 97.1 us
  local copies, waits for them, and re-layouts: 106 us -> 13.8 us
  Pallas kernels: 0 us -> 80.8 us
  blocking collectives: 59.6 us -> 0 us
  matrix products: 54 us -> 0 us
  other arithmetic: 36.4 us -> 1.82 us
  starting transfers between devices: 22.9 us -> 0 us
  waiting for transfers between devices: 22.9 us -> 0 us
    pallas_call x0 -> x3, Pallas kernels: none -> 80.8 us  [the longest x1 38.5 us: finish_part(): pl.pallas_call(functools.partial(finish_kernel, with_video), out_shape=tu...]
    all_to_all x5 -> x0, blocking collectives: 59.6 us -> none  [the longest x2 30.6 us: copy_for_each(): lax.all_to_all(jnp.broadcast_to(x[None], (devices, *x.shape)), axis, 0, 0...]
    dot_general x18 -> x0, matrix products: 54 us -> none  [the longest x4 23.6 us: audio_block(): jnp.einsum('ahd,bhd->ahb', audio_q, key, preferred_element_type=jnp.float32)]
    another operation x3 -> x0, local copies, waits for them, and re-layouts: 27.9 us -> none  [the longest x1 11.6 us: shards(): value_blocks = video_kv[1].reshape(blocks, block, heads, HD)]
    reduce_sum x9 -> x0, other arithmetic: 24.3 us -> none  [the longest x4 18.4 us: audio_block(): total = total * factor + jnp.sum(weights, axis=2)]
    all_to_all x4 -> x0, starting transfers between devices: 22.9 us -> none  [the longest x2 9.58 us: copy_for_each(): lax.all_to_all(jnp.broadcast_to(x[None], (devices, *x.shape)), axis, 0, 0...]
    all_to_all x4 -> x0, waiting for transfers between devices: 22.9 us -> none  [the longest x1 22.9 us: summed_rows(): lax.all_to_all(nearer, far, split_axis=0, concat_axis=0, tiled=True)]
    while x23 -> x0, local copies, waits for them, and re-layouts: 17.3 us -> none  [the longest x3 12.4 us: shards(): lax.map(video_block, (query_blocks, clip_blocks)).reshape(local_rows, width)]
  transfers between devices with their start and end apart: 4 -> 0, of which waited for: 1 -> 0; matrix products, arithmetic and copies ran while one was open for 34% -> 0% of each run, Pallas kernels for 0% -> 0%
where the time goes in v1:
time: 97.4 us; the launch traced here: 97.1 us
  Pallas kernels  80.8 us (83%)
  local copies, waits for them, and re-layouts  13.8 us (14%)
  other arithmetic  1.82 us (2%)
    pallas_call x1, Pallas kernels, finish_part(): pl.pallas_call(functools.partial(finish_kernel, with_video), out_shape=tu...  38.5 us
    pallas_call x1, Pallas kernels, project(): pl.pallas_call(project_kernel, out_shape=jax.ShapeDtypeStruct((4, 256, 76...  30.3 us
    unnamed x12, local copies, waits for them, and re-layouts  13.1 us
    pallas_call x1, Pallas kernels, audio_part(): pl.pallas_call(audio_kernel, out_shape=(jax.ShapeDtypeStruct((256, 1024),...  12 us

profile of v1, /device:TPU:0, one launch (start us, length us, event | category | flops | bytes accessed | tf_op | source)
XLA Modules:
  0.0 97.1 jit_solution(6895342983026166558)
XLA Ops:
  0.6 0.8 select_convert_fusion.mask
  1.4 1.0 %copy.9.wout = bf16[1024,32]{1,0:T(8,128)(2,1)S(1)} copy(bf16[1024,32]{0,1:T(8,128)(2,1)} %param.13) | data formatting | bytes 131072 | tf_op args[6]
  2.4 1.0 %fusion.hot = bf16[2048,128]{1,0:T(8,128)(2,1)S(1)} fusion(s32[2048]{0:T(1024)} %param.9), kind=kLoop, calls=%fused_computation.1 | loop fusion | flops 524288 | bytes 532480 | tf_op jit(solution)/shard_map/convert_element_type | solution.py:473
  3.5 0.0 copy-start.3
  3.5 1.2 %copy-done.3 = bf16[256,2048]{1,0:T(8,128)(2,1)S(1)} copy-done((bf16[256,2048]{1,0:T(8,128)(2,1)S(1)}, bf16[256,2048]{1,0:T(8,128)(2,1)}, u32[]{:S(2)}) %copy-start.3) | copy-done | bytes 1048600
  4.7 0.0 copy-start.4
  4.7 0.9 copy-done.4
  5.6 30.3 %shard_map.86.qkv = bf16[4,256,768]{2,1,0:T(8,128)(2,1)S(1)} custom-call(bf16[256,2048]{1,0:T(8,128)(2,1)S(1)} %copy-done.3, bf16[1,128,768]{2,1,0:T(8,128)(2,1)S(1)} %copy-done.4), custom_call_target="tpu_custom_call" | custom-call | tf_op jit(solution)/shard_map/pallas_call | solution.py:154
  36.0 0.0 copy-start
  36.0 3.4 %copy-done = bf16[2,2048,1024]{2,1,0:T(8,128)(2,1)S(1)} copy-done((bf16[2,2048,1024]{2,1,0:T(8,128)(2,1)S(1)}, bf16[2,2048,1024]{2,1,0:T(8,128)(2,1)}, u32[]{:S(2)}) %copy-start) | copy-done | bytes 8388632
  39.4 0.0 copy-start.2
  39.4 12.0 %shard_map.87 = (f32[256,1024]{1,0:T(8,128)S(1)}, f32[256,128]{1,0:T(8,128)S(1)}) custom-call(bf16[4,256,768]{2,1,0:T(8,128)(2,1)S(1)} %shard_map.86.qkv, bf16[256,128]{1,0:T(8,128)(2,1)S(1)} %select_convert_fusion.mask, bf16[2048,128]{1,0:T(8,128)(2,1)S(1)} %fusion.hot, bf16[2,2048,1024]{2,1,0:T(8,128)(2,1)S(1)} %copy-done), custom_call_target="tpu_custom_call" | custom-call | tf_op jit(solution)/shard_map/pallas_call | solution.py:256
  51.3 0.0 copy-done.2
  51.3 38.5 %shard_map.88 = (bf16[2048,1024]{1,0:T(8,128)(2,1)S(1)}, bf16[128,32]{1,0:T(8,128)(2,1)S(1)}) custom-call(f32[256,1024]{1,0:T(8,128)S(1)} %get-tuple-element.4.numer, f32[256,128]{1,0:T(8,128)S(1)} %get-tuple-element.5.stat, bf16[1024,32]{1,0:T(8,128)(2,1)S(1)} %copy.9.wout, bf16[4,256,768]{2,1,0:T(8,128)(2,1)S(1)} %shard_map.86.qkv, ...), custom_call_target="tpu_custom_call" | custom-call | tf_op jit(solution)/shard_map/pallas_call | solution.py:440
  89.8 0.0 copy-start.1
  89.8 1.9 %copy-done.1 = bf16[2048,1024]{1,0:T(8,128)(2,1)} copy-done((bf16[2048,1024]{1,0:T(8,128)(2,1)}, bf16[2048,1024]{1,0:T(8,128)(2,1)S(1)}, u32[]{:S(2)}) %copy-start.1) | copy-done | bytes 4194328
  91.8 0.7 copy.10
  92.4 4.6 %copy.12 = bf16[2048,1024]{1,0:T(8,128)(2,1)} copy(bf16[2048,1024]{1,0:T(8,128)(2,1)} %copy-done.1) | data formatting | bytes 8388608
  (1 shorter events, 0.0 us)
Async XLA Ops:
  3.5 1.2 %copy-start.3 = (bf16[256,2048]{1,0:T(8,128)(2,1)S(1)}, bf16[256,2048]{1,0:T(8,128)(2,1)}, u32[]{:S(2)}) copy-start(bf16[256,2048]{1,0:T(8,128)(2,1)} %x.1) | copy-start | bytes 3145732
  4.7 0.9 copy-start.4
  36.0 3.4 %copy-start = (bf16[2,2048,1024]{2,1,0:T(8,128)(2,1)S(1)}, bf16[2,2048,1024]{2,1,0:T(8,128)(2,1)}, u32[]{:S(2)}) copy-start(bf16[2,2048,1024]{2,1,0:T(8,128)(2,1)} %kv.1) | copy-start | bytes 25165828
  39.4 12.0 %copy-start.2 = (bf16[2048,1024]{1,0:T(8,128)(2,1)S(1)}, bf16[2048,1024]{1,0:T(8,128)(2,1)}, u32[]{:S(2)}) copy-start(bf16[2048,1024]{1,0:T(8,128)(2,1)} %vq.1) | copy-start | bytes 12582916
  89.8 1.9 %copy-start.1 = (bf16[2048,1024]{1,0:T(8,128)(2,1)}, bf16[2048,1024]{1,0:T(8,128)(2,1)S(1)}, u32[]{:S(2)}) copy-start(bf16[2048,1024]{1,0:T(8,128)(2,1)S(1)} %get-tuple-element.10) | copy-start | bytes 12582916

commit v2 on v0

v2 whole, which is shorter than its diff:
```python
import functools

import jax
import jax.numpy as jnp
from jax import lax
from jax.experimental import pallas as pl
from jax.experimental.pallas import tpu as pltpu
from jax.sharding import PartitionSpec as P

F32 = jnp.float32
BF = jnp.bfloat16
NT = (((1,), (1,)), ((), ()))
BIG = -1e30
MESH = pl.DeviceIdType.MESH
VMEM = pl.BlockSpec(memory_space=pltpu.VMEM)
ANY = pl.BlockSpec(memory_space=pl.ANY)
CHIPS = 32
GROUP = 8
QUARTERS = 4
WITHIN = 6
SIZE = 512


def lanes(j, width=128):
    return pl.ds(pl.multiple_of(j * width, width), width)


def rows_of(at, n):
    return pl.ds(pl.multiple_of(at, 16), n)


def remote(src, dst, send, recv, chip, core, head):
    return pltpu.make_async_remote_copy(
        src_ref=src,
        dst_ref=dst,
        send_sem=send,
        recv_sem=recv,
        device_id=(chip * 2 + core, head),
        device_id_type=MESH,
    )


def one_hot(clip, count):
    row = lax.broadcasted_iota(jnp.int32, (128, 128), 0)
    return [row == jnp.broadcast_to(clip[t : t + 1, :], (128, 128)) for t in range(count)]


def clip_mask(aclip):
    row = lax.broadcasted_iota(jnp.int32, (128, 128), 0)
    tiles = [jnp.where(same | (row >= 8), 0.0, BIG) for same in one_hot(aclip, 2)]
    return jnp.concatenate(tiles, 1)


def fill_hot(hot, vclip):
    for t, same in enumerate(one_hot(vclip, 16)):
        hot[t * 128 : (t + 1) * 128, :] = jnp.where(same, 1.0, 0.0).T.astype(BF)


def video_pair(kt, vt, mask_t, hot, vq, vout, at):
    size = 1024
    lane = lax.broadcasted_iota(jnp.int32, (size, 128), 1)
    row = lax.broadcasted_iota(jnp.int32, (128, 256), 0)
    scaled = (kt.astype(F32) * 0.125).astype(BF)
    zero = jnp.zeros_like(scaled)
    first = jnp.concatenate([jnp.where(row < 64, scaled, zero), mask_t], 0)
    second = jnp.concatenate([jnp.where(row >= 64, scaled, zero), mask_t], 0)
    keys = jnp.concatenate([first, second], 1)
    values = jnp.concatenate([vt, jnp.ones((128, 256), BF)], 0)
    for c in range(vq.shape[0] // size):
        rows = pl.ds(c * size, size)
        q = jnp.concatenate([vq[rows, at], hot[rows, :]], 1)
        s = jnp.dot(q, keys, preferred_element_type=F32)
        r = []
        for h in range(2):
            sh = s[:, h * 256 : (h + 1) * 256]
            p = jnp.exp(sh - jnp.max(sh, axis=1, keepdims=True)).astype(BF)
            r.append(lax.dot_general(p, values, NT, preferred_element_type=F32))
        num = jnp.where(lane < 64, r[0][:, :128], r[1][:, :128])
        den = jnp.where(lane < 64, r[0][:, 128:], r[1][:, 128:])
        vout[rows, at] = (num / den).astype(BF)


def widened(f, first, count):
    n = f.shape[0]
    lane = lax.broadcasted_iota(jnp.int32, (n, 128), 1)
    out = []
    for p in range(first, first + count, 2):
        a = jnp.broadcast_to(f[:, p : p + 1], (n, 128))
        b = jnp.broadcast_to(f[:, p + 1 : p + 2], (n, 128))
        out.append(jnp.where(lane < 64, a, b))
    return jnp.concatenate(out, 1)


def gather(part, mine, full, n, local, send_sem, recv_sem, pass_send, pass_recv, where):
    quarter, g, chip, core, head = where

    def block(q, k, i):
        return full.at[rows_of(((q * 2 + k) * GROUP + i) * n, n)]

    def group(q, k):
        return full.at[rows_of((q * 2 + k) * GROUP * n, GROUP * n)]

    own = block(quarter, core, g)

    def begin():
        pltpu.make_async_copy(mine, own, recv_sem.at[quarter]).start()

        def one(i, _):
            q = lax.rem(quarter + i // GROUP, QUARTERS)
            to = q * GROUP + lax.rem(g + i, GROUP)
            remote(mine, own, send_sem, recv_sem.at[quarter], to, core, head).start()
            return 0

        lax.fori_loop(1, CHIPS, one, 0)

    def relay(q):
        blocks = group(q, core)
        remote(blocks, blocks, send_sem, recv_sem.at[q], chip, 1 - core, head).wait_recv()
        remote(blocks, blocks, pass_send.at[q], pass_recv.at[q], chip, 1 - core, head).start()

    def passed(q):
        blocks = group(q, 1 - core)
        remote(blocks, blocks, pass_send.at[q], pass_recv.at[q], chip, 1 - core, head).wait_recv()

    def end():
        for q in range(QUARTERS):
            blocks = group(q, core)
            remote(
                blocks, blocks, pass_send.at[q], pass_recv.at[q], chip, 1 - core, head
            ).wait_send()
        sent = full.at[pl.ds(0, (CHIPS - 1) * n)]
        remote(sent, sent, send_sem, recv_sem.at[0], chip, 1 - core, head).wait_send()

    return begin, relay, passed, end


def main_kernel(
    x, w, vclip, aclip, kv, vq, wout,
    vout, tail, out,
    xs, ks, vs, qs, os, wt, wl, mine, qkv, hot, mask, mask_t,
    sa, sb, ma, mb, numer, stat, near_n, near_s, comb, land, attn, gath, part, swap, back,
    local, pair_out, one, bar1, bar2, bar3, bar4, bar5, bar6, bar7, bar8,
):
    seq, head = lax.axis_index("seq"), lax.axis_index("head")
    chip, core = seq // 2, seq % 2
    quarter, g = chip // GROUP, chip % GROUP
    where = (quarter, g, chip, core, head)

    load_x = pltpu.make_async_copy(x, xs, local.at[0])
    load_k = pltpu.make_async_copy(kv.at[0], ks, local.at[1])
    load_v = pltpu.make_async_copy(kv.at[1], vs, local.at[2])
    load_q = pltpu.make_async_copy(vq, qs, local.at[3])
    load_x.start()

    barrier = pltpu.get_barrier_semaphore()

    def greet(c, k, h):
        pl.semaphore_signal(barrier, inc=1, device_id=(c * 2 + k, h), device_id_type=MESH)

    def greet_chip(i, _):
        greet(lax.rem(chip + i, CHIPS), core, head)
        return 0

    def greet_near(i, _):
        greet(quarter * GROUP + lax.rem(g + i, GROUP), 1 - core, head)
        return 0

    lax.fori_loop(0, GROUP, greet_near, 0)
    lax.fori_loop(1, CHIPS, greet_chip, 0)
    greet(chip, core, 1 - head)
    load_k.start()
    load_v.start()
    load_q.start()
    wt[...] = w[0].astype(F32).T.astype(BF)
    pl.semaphore_wait(barrier, GROUP + CHIPS)

    feature = g * 2 + core

    def weights_to(i):
        to, k = lax.rem(g + i // 2, GROUP), lax.rem(core + i, 2)
        rows = wt.at[rows_of((k * GROUP + to) * 48, 48)]
        return remote(rows, wl.at[feature], one.at[0], one.at[1], quarter * GROUP + to, k, head)

    def weights_start(i, _):
        weights_to(i).start()
        return 0

    own_w = pltpu.make_async_copy(
        wt.at[rows_of((core * GROUP + g) * 48, 48)], wl.at[feature], one.at[1]
    )
    own_w.start()
    lax.fori_loop(1, 2 * GROUP, weights_start, 0)
    fill_hot(hot, vclip)
    flat = clip_mask(aclip)
    mask_t[...] = flat.astype(BF)
    mask[...] = flat.T.astype(BF)
    load_x.wait()
    remote(wl, wl, one.at[0], one.at[1], chip, 1 - core, head).wait_recv()
    columns = jnp.concatenate([wl[f] for f in range(2 * GROUP)], 1)
    mine[...] = lax.dot_general(columns, xs[...], NT, preferred_element_type=F32).astype(BF)

    begin, relay, passed, end_first = gather(
        None, mine, qkv, 48, None, one.at[2], bar1, bar2, bar3, where
    )

    @pl.when(quarter < 2)
    def _():
        begin()

    relay(0)
    relay(1)

    @pl.when(quarter >= 2)
    def _():
        begin()

    load_k.wait()
    load_v.wait()
    passed(0)
    passed(1)

    pieces = ks.shape[0] // SIZE
    lane = lax.broadcasted_iota(jnp.int32, (256, 128), 1)
    ones = jnp.ones((SIZE, 128), BF)
    stat[...] = jnp.zeros_like(stat)

    def pair_of(jj):
        return lax.rem(jj + 4 * (1 - core), 8)

    def query(jj):
        q = (qkv[lanes(pair_of(jj)), :].astype(F32) * 0.125).T
        zero = jnp.zeros_like(q)
        first = jnp.concatenate([jnp.where(lane < 64, q, zero).astype(BF), mask[...]], 1)
        second = jnp.concatenate([jnp.where(lane >= 64, q, zero).astype(BF), mask[...]], 1)
        return jnp.concatenate([first, second], 0)

    def score(jj, q2, c, s_ref, top):
        rows = pl.ds(c * SIZE, SIZE)
        keys = jnp.concatenate([ks[rows, lanes(pair_of(jj))], hot[rows, :]], 1)
        s = lax.dot_general(q2, keys, NT, preferred_element_type=F32)
        s_ref[:, c * SIZE : (c + 1) * SIZE] = s
        for t in range(SIZE // 128):
            piece = s[:, t * 128 : (t + 1) * 128]
            top = piece if top is None else jnp.maximum(top, piece)
        return top

    def keep(top, m_ref):
        m_ref[...] = jnp.broadcast_to(jnp.max(top, axis=1, keepdims=True), (512, 128))

    def weigh(jj, top, c, s_ref, acc):
        rows = pl.ds(c * SIZE, SIZE)
        wide = jnp.concatenate([top] * (SIZE // 128), 1)
        weights = jnp.exp(s_ref[:, c * SIZE : (c + 1) * SIZE] - wide).astype(BF)
        values = jnp.concatenate([vs[rows, lanes(pair_of(jj))], ones], 1)
        r = jnp.dot(weights, values, preferred_element_type=F32)
        return r if acc is None else acc + r

    def step(jj, half, following, s_ref, m_ref, s_next, m_next):
        q2 = query(following)
        top, acc, now = None, None, m_ref[...]
        for c in range(pieces):
            top = score(following, q2, c, s_next, top)
            acc = weigh(jj, now, c, s_ref, acc)
        keep(top, m_next)
        numer[half, :, lanes(jj - 4 * half)] = jnp.where(
            lane < 64, acc[:256, :128], acc[256:, :128]
        )
        st, at = stat[half], 2 * (jj - 4 * half)
        st = jnp.where(lane == at, now[:256], st)
        st = jnp.where(lane == at + 1, now[256:], st)
        st = jnp.where(lane == at + 64, acc[:256, 128:], st)
        stat[half] = jnp.where(lane == at + 65, acc[256:, 128:], st)

    def two(half, i, _):
        jj = 4 * half + 2 * i
        step(jj, half, jj + 1, sa, ma, sb, mb)
        step(jj + 1, half, jnp.minimum(jj + 2, 7), sb, mb, sa, ma)
        return 0

    q2, top = query(0), None
    for c in range(pieces):
        top = score(0, q2, c, sa, top)
    keep(top, ma)
    lax.fori_loop(0, 2, functools.partial(two, 0), 0)
    send_n = remote(numer.at[0], near_n, one.at[3], one.at[4], chip, 1 - core, head)
    send_s = remote(stat.at[0], near_s, one.at[5], one.at[6], chip, 1 - core, head)
    send_n.start()
    send_s.start()
    relay(2)
    relay(3)
    lax.fori_loop(0, 2, functools.partial(two, 1), 0)

    send_s.wait_recv()
    send_n.wait_recv()
    a, b = stat[1], near_s[...]
    top = jnp.maximum(a, b)
    high = top.astype(BF).astype(F32)
    top = high + (top - high).astype(BF).astype(F32)
    fa = jnp.where(lane < 64, jnp.exp(a - top), 0.0)
    fb = jnp.where(lane < 64, jnp.exp(b - top), 0.0)
    st = jnp.where(lane < 64, top, a * pltpu.roll(fa, 64, 1) + b * pltpu.roll(fb, 64, 1))
    high = st.astype(BF).astype(F32)
    both = numer[1] * widened(fa, 0, 8) + near_n[...] * widened(fb, 0, 8)

    def stacked(u, v):
        return jnp.concatenate(
            [u.reshape(CHIPS, 8, u.shape[1]), v.reshape(CHIPS, 8, v.shape[1])], 1
        ).astype(BF)

    comb[:, :, :256] = stacked(both[:, :256], both[:, 256:])
    comb[:, :, 256:] = stacked(high, st - high)

    def scatter_start(i, _):
        to = lax.rem(chip + i, CHIPS)
        remote(comb.at[to], land.at[i], one.at[7], one.at[8], to, core, head).start()
        return 0

    lax.fori_loop(1, CHIPS, scatter_start, 0)
    land[0] = comb[chip]

    load_q.wait()
    passed(2)
    passed(3)

    def video(j0, j1):
        def pair(j, _):
            video_pair(
                qkv[lanes(j + 8), :], qkv[lanes(j + 16), :], mask_t[...], hot, qs, os, lanes(j)
            )
            pltpu.make_async_copy(
                os.at[:, lanes(j)], vout.at[:, lanes(j)], pair_out.at[j]
            ).start()
            return 0

        lax.fori_loop(j0, j1, pair, 0)

    rest = 128 * (8 - WITHIN)
    tail[:rest, :] = qkv[1024 + 128 * WITHIN : 2048, :]
    tail[rest:, :] = qkv[2048 + 128 * WITHIN : 3072, :]
    video(0, 3)

    others = land.at[pl.ds(1, CHIPS - 1)]
    remote(others, others, one.at[7], one.at[8], chip, 1 - core, head).wait_recv()
    arrived = land[:, :, 256:].astype(F32)
    st = arrived[:, :8] + arrived[:, 8:]
    small = lax.broadcasted_iota(jnp.int32, (8, 128), 1)
    top = jnp.max(st, axis=0)
    total = jnp.zeros((16, 256), F32)
    den = jnp.zeros((8, 128), F32)
    for i in range(CHIPS):
        f = jnp.where(small < 64, jnp.exp(st[i] - top), 0.0)
        den = den + st[i] * pltpu.roll(f, 64, 1)
        scale = jnp.concatenate([widened(f, 0, 4), widened(f, 4, 4)], 0)
        total = total + land[i, :, :256].astype(F32) * scale
    scale = jnp.concatenate([widened(den, 64, 4), widened(den, 68, 4)], 0)
    attn[...] = (total / scale).astype(BF)

    begin, relay, passed, end_second = gather(
        None, attn, gath, 16, None, one.at[9], bar4, bar5, bar6, where
    )
    begin()
    video(3, 5)
    for q in range(QUARTERS):
        relay(q)
    video(5, 6)
    for q in range(QUARTERS):
        passed(q)
    acc = None
    for k in range(2):
        groups = [
            gath[(q * 2 + k) * GROUP * 16 : (q * 2 + k + 1) * GROUP * 16, :]
            for q in range(QUARTERS)
        ]
        rows = jnp.concatenate(groups, 0)
        for h in range(2):
            at = k * 512 + h * 256
            r = lax.dot_general(rows, wout[:, at : at + 256], NT, preferred_element_type=F32)
            r = r.reshape(CHIPS, 16, 32)[:, h * 8 : (h + 1) * 8]
            acc = r if acc is None else acc + r
    flat = acc.reshape(256, 32).T
    part[0] = flat[:, :128]
    part[1] = flat[:, 128:]
    across = remote(part.at[1 - head], back, one.at[10], one.at[11], chip, core, 1 - head)
    across.start()
    video(6, WITHIN)
    across.wait_recv()
    out[...] = (part[head] + back[...]).astype(BF)

    across.wait_send()
    end_first()
    end_second()
    remote(others, others, one.at[7], one.at[8], chip, 1 - core, head).wait_send()
    send_n.wait_send()
    send_s.wait_send()
    weights = wl.at[pl.ds(0, 2 * GROUP - 1)]
    remote(weights, weights, one.at[0], one.at[1], chip, 1 - core, head).wait_send()
    for j in range(WITHIN):
        pltpu.make_async_copy(os.at[:, lanes(j)], vout.at[:, lanes(j)], pair_out.at[j]).wait()


def main_part(x, w, vclip, aclip, kv, vq, wout):
    n = vq.shape[0]
    dma = pltpu.SemaphoreType.DMA
    return pl.pallas_call(
        main_kernel,
        out_shape=(
            jax.ShapeDtypeStruct((n, 128 * WITHIN), BF),
            jax.ShapeDtypeStruct((256 * (8 - WITHIN), 256), BF),
            jax.ShapeDtypeStruct((32, 128), BF),
        ),
        in_specs=[ANY, VMEM, VMEM, VMEM, ANY, ANY, VMEM],
        out_specs=(ANY, VMEM, VMEM),
        scratch_shapes=[
            pltpu.VMEM((256, 2048), BF),
            pltpu.VMEM((n, 1024), BF),
            pltpu.VMEM((n, 1024), BF),
            pltpu.VMEM((n, 1024), BF),
            pltpu.VMEM((n, 128 * WITHIN), BF),
            pltpu.VMEM((768, 128), BF),
            pltpu.VMEM((16, 48, 128), BF),
            pltpu.VMEM((48, 256), BF),
            pltpu.VMEM((3072, 256), BF),
            pltpu.VMEM((n, 128), BF),
            pltpu.VMEM((256, 128), BF),
            pltpu.VMEM((128, 256), BF),
            pltpu.VMEM((512, n), F32),
            pltpu.VMEM((512, n), F32),
            pltpu.VMEM((512, 128), F32),
            pltpu.VMEM((512, 128), F32),
            pltpu.VMEM((2, 256, 512), F32),
            pltpu.VMEM((2, 256, 128), F32),
            pltpu.VMEM((256, 512), F32),
            pltpu.VMEM((256, 128), F32),
            pltpu.VMEM((CHIPS, 16, 384), BF),
            pltpu.VMEM((CHIPS, 16, 384), BF),
            pltpu.VMEM((16, 256), BF),
            pltpu.VMEM((1024, 256), BF),
            pltpu.VMEM((2, 32, 128), F32),
            pltpu.VMEM((8, 128), F32),
            pltpu.VMEM((32, 128), F32),
            dma((4,)),
            dma((WITHIN,)),
            dma((12,)),
        ]
        + [dma((QUARTERS,))] * 8,
        compiler_params=pltpu.CompilerParams(
            collective_id=0, has_side_effects=True, vmem_limit_bytes=52 * 2**20
        ),
    )(x, w, vclip, aclip, kv, vq, wout)


def tail_kernel(tail, aclip, vclip, vq, first, projected, vout, out, hot, qs, os, sem):
    move = pltpu.make_async_copy(first, vout.at[:, pl.ds(0, 128 * WITHIN)], sem.at[0])
    load = pltpu.make_async_copy(
        vq.at[:, pl.ds(128 * WITHIN, 128 * (8 - WITHIN))], qs, sem.at[1]
    )
    load.start()
    move.start()
    out[...] = projected[...]
    fill_hot(hot, vclip)
    mask_t = clip_mask(aclip).astype(BF)
    load.wait()
    rest = 128 * (8 - WITHIN)
    for j in range(8 - WITHIN):
        at = slice(j * 128, (j + 1) * 128)
        keys, values = tail[at, :], tail[rest + j * 128 : rest + (j + 1) * 128, :]
        video_pair(keys, values, mask_t, hot, qs, os, at)
        pltpu.make_async_copy(
            os.at[:, at], vout.at[:, pl.ds(128 * (WITHIN + j), 128)], sem.at[2 + j]
        ).start()
    for j in range(8 - WITHIN):
        at = slice(j * 128, (j + 1) * 128)
        pltpu.make_async_copy(
            os.at[:, at], vout.at[:, pl.ds(128 * (WITHIN + j), 128)], sem.at[2 + j]
        ).wait()
    move.wait()


def tail_part(tail, aclip, vclip, vq, first, projected):
    n = vq.shape[0]
    return pl.pallas_call(
        tail_kernel,
        out_shape=(jax.ShapeDtypeStruct(vq.shape, BF), jax.ShapeDtypeStruct((32, 128), BF)),
        in_specs=[VMEM, VMEM, VMEM, ANY, ANY, VMEM],
        out_specs=(ANY, VMEM),
        scratch_shapes=[
            pltpu.VMEM((n, 128), BF),
            pltpu.VMEM((n, 128 * (8 - WITHIN)), BF),
            pltpu.VMEM((n, 128 * (8 - WITHIN)), BF),
            pltpu.SemaphoreType.DMA((10 - WITHIN,)),
        ],
        compiler_params=pltpu.CompilerParams(vmem_limit_bytes=40 * 2**20),
    )(tail, aclip, vclip, vq, first, projected)


def shards(vq, kv, video_clip, x, w, audio_clip, wout):
    vclip = video_clip.reshape(-1, 128)
    aclip = audio_clip.reshape(-1, 128)
    first, tail, projected = main_part(x, w, vclip, aclip, kv, vq, wout.T)
    video_attn, out = tail_part(tail, aclip, vclip, vq, first, projected)
    return video_attn, out.T


def solution(mesh):
    return jax.shard_map(
        shards,
        mesh=mesh,
        in_specs=(
            P("seq", "head"),
            P(None, "seq", "head"),
            P("seq"),
            P(),
            P("seq", None, "head"),
            P(),
            P("head", "seq"),
        ),
        out_specs=(P("seq", "head"), P("head", "seq")),
        check_vma=False,
    )
```

time: 307 us -> 74.9 us (0.24); the launches traced: 303 us -> 74.6 us
  local copies, waits for them, and re-layouts: 106 us -> 6.24 us
  Pallas kernels: 0 us -> 67.5 us
  blocking collectives: 59.6 us -> 0 us
  matrix products: 54 us -> 0 us
  other arithmetic: 36.4 us -> 0 us
  starting transfers between devices: 22.9 us -> 0 us
  waiting for transfers between devices: 22.9 us -> 0 us
    pallas_call x0 -> x2, Pallas kernels: none -> 67.5 us  [the longest x1 62.9 us: main_part(): pl.pallas_call(main_kernel, out_shape=(jax.ShapeDtypeStruct((n, 128 * WIT...]
    all_to_all x5 -> x0, blocking collectives: 59.6 us -> none  [the longest x2 30.6 us: copy_for_each(): lax.all_to_all(jnp.broadcast_to(x[None], (devices, *x.shape)), axis, 0, 0...]
    dot_general x18 -> x0, matrix products: 54 us -> none  [the longest x4 23.6 us: audio_block(): jnp.einsum('ahd,bhd->ahb', audio_q, key, preferred_element_type=jnp.float32)]
    another operation x3 -> x0, local copies, waits for them, and re-layouts: 27.9 us -> none  [the longest x1 11.6 us: shards(): value_blocks = video_kv[1].reshape(blocks, block, heads, HD)]
    reduce_sum x9 -> x0, other arithmetic: 24.3 us -> none  [the longest x4 18.4 us: audio_block(): total = total * factor + jnp.sum(weights, axis=2)]
    all_to_all x4 -> x0, starting transfers between devices: 22.9 us -> none  [the longest x2 9.58 us: copy_for_each(): lax.all_to_all(jnp.broadcast_to(x[None], (devices, *x.shape)), axis, 0, 0...]
    all_to_all x4 -> x0, waiting for transfers between devices: 22.9 us -> none  [the longest x1 22.9 us: summed_rows(): lax.all_to_all(nearer, far, split_axis=0, concat_axis=0, tiled=True)]
    while x23 -> x0, local copies, waits for them, and re-layouts: 17.3 us -> none  [the longest x3 12.4 us: shards(): lax.map(video_block, (query_blocks, clip_blocks)).reshape(local_rows, width)]
  transfers between devices with their start and end apart: 4 -> 0, of which waited for: 1 -> 0; matrix products, arithmetic and copies ran while one was open for 34% -> 0% of each run, Pallas kernels for 0% -> 0%
where the time goes in v2:
time: 74.9 us; the launch traced here: 74.6 us
  Pallas kernels  67.5 us (90%)
  local copies, waits for them, and re-layouts  6.24 us (8%)
  between operations  0.83 us (1%)
    pallas_call x1, Pallas kernels, main_part(): pl.pallas_call(main_kernel, out_shape=(jax.ShapeDtypeStruct((n, 128 * WIT...  62.9 us
    unnamed x14, local copies, waits for them, and re-layouts  6.24 us
    pallas_call x1, Pallas kernels, tail_part(): pl.pallas_call(tail_kernel, out_shape=(jax.ShapeDtypeStruct(vq.shape, BF)...  4.59 us

profile of v2, /device:TPU:0, one launch (start us, length us, event | category | flops | bytes accessed | tf_op | source)
XLA Modules:
  0.0 74.6 jit_solution(11562178856070632542)
XLA Ops:
  0.6 0.0 copy-start.2
  0.6 1.2 %copy-done.2 = bf16[256,2048]{1,0:T(8,128)(2,1)S(1)} copy-done((bf16[256,2048]{1,0:T(8,128)(2,1)S(1)}, bf16[256,2048]{1,0:T(8,128)(2,1)}, u32[]{:S(2)}) %copy-start.2) | copy-done | bytes 1048600
  1.9 0.0 copy-start.3
  1.9 0.9 %copy-done.3 = bf16[1,128,768]{2,1,0:T(8,128)(2,1)S(1)} copy-done((bf16[1,128,768]{2,1,0:T(8,128)(2,1)S(1)}, bf16[1,128,768]{2,1,0:T(8,128)(2,1)}, u32[]{:S(2)}) %copy-start.3) | copy-done | bytes 196632
  2.8 0.0 copy-start.4
  2.8 0.8 %copy-done.4 = bf16[1024,32]{0,1:T(8,128)(2,1)S(1)} copy-done((bf16[1024,32]{0,1:T(8,128)(2,1)S(1)}, bf16[1024,32]{0,1:T(8,128)(2,1)}, u32[]{:S(2)}) %copy-start.4) | copy-done | bytes 65560
  3.6 0.0 copy-start.5
  3.6 0.7 copy-done.5
  4.3 0.0 copy-start.6
  4.3 0.7 copy-done.6
  5.0 0.0 copy-start
  5.0 62.9 %shard_map.86 = (bf16[2048,768]{1,0:T(8,128)(2,1)}, bf16[512,256]{1,0:T(8,128)(2,1)S(1)}, bf16[32,128]{1,0:T(8,128)(2,1)S(1)}) custom-call(bf16[256,2048]{1,0:T(8,128)(2,1)S(1)} %copy-done.2, bf16[1,128,768]{2,1,0:T(8,128)(2,1)S(1)} %copy-done.3, s32[16,128]{1,0:T(8,128)S(1)} %bitcast.5, s32[2,128]{1,0:T(2,128)S(1)} %bitcast.7, bf16[2,2048,1024]{2,1,0:T(8,128)(2,1)} %kv.1, ...), custom_call_target="tpu_custom_call" | custom-call | tf_op jit(solution)/shard_map/pallas_call | solution.py:404
  67.9 0.0 copy-done
  68.0 0.0 copy-start.1
  68.0 1.9 %copy-done.1 = bf16[2048,768]{1,0:T(8,128)(2,1)S(1)} copy-done((bf16[2048,768]{1,0:T(8,128)(2,1)S(1)}, bf16[2048,768]{1,0:T(8,128)(2,1)}, u32[]{:S(2)}) %copy-start.1) | copy-done | bytes 3145752
  69.8 4.6 %shard_map.87 = (bf16[2048,1024]{1,0:T(8,128)(2,1)}, bf16[32,128]{1,0:T(8,128)(2,1)}) custom-call(bf16[512,256]{1,0:T(8,128)(2,1)S(1)} %get-tuple-element.7.tail, s32[2,128]{1,0:T(2,128)S(1)} %bitcast.8, s32[16,128]{1,0:T(8,128)S(1)} %bitcast.6, bf16[2048,1024]{1,0:T(8,128)(2,1)S(1)} %copy-done, bf16[2048,768]{1,0:T(8,128)(2,1)S(1)} %copy-done.1, ...), custom_call_target="tpu_custom_call" | custom-call | tf_op jit(solution)/shard_map/pallas_call | solution.py:481
Async XLA Ops:
  0.6 1.2 %copy-start.2 = (bf16[256,2048]{1,0:T(8,128)(2,1)S(1)}, bf16[256,2048]{1,0:T(8,128)(2,1)}, u32[]{:S(2)}) copy-start(bf16[256,2048]{1,0:T(8,128)(2,1)} %x.1) | copy-start | bytes 3145732
  1.9 0.9 %copy-start.3 = (bf16[1,128,768]{2,1,0:T(8,128)(2,1)S(1)}, bf16[1,128,768]{2,1,0:T(8,128)(2,1)}, u32[]{:S(2)}) copy-start(bf16[1,128,768]{2,1,0:T(8,128)(2,1)} %w.1) | copy-start | bytes 589828
  2.8 0.8 %copy-start.4 = (bf16[1024,32]{0,1:T(8,128)(2,1)S(1)}, bf16[1024,32]{0,1:T(8,128)(2,1)}, u32[]{:S(2)}) copy-start(bf16[1024,32]{0,1:T(8,128)(2,1)} %param.13) | copy-start | bytes 196612
  3.6 0.7 copy-start.5
  4.3 0.7 copy-start.6
  5.0 62.9 %copy-start = (bf16[2048,1024]{1,0:T(8,128)(2,1)S(1)}, bf16[2048,1024]{1,0:T(8,128)(2,1)}, u32[]{:S(2)}) copy-start(bf16[2048,1024]{1,0:T(8,128)(2,1)} %vq.3) | copy-start | bytes 12582916
  68.0 1.9 %copy-start.1 = (bf16[2048,768]{1,0:T(8,128)(2,1)S(1)}, bf16[2048,768]{1,0:T(8,128)(2,1)}, u32[]{:S(2)}) copy-start(bf16[2048,768]{1,0:T(8,128)(2,1)} %get-tuple-element.8.first) | copy-start | bytes 9437188

commit v3 on v2

--- a/solution.py
+++ b/solution.py
@@ -13,11 +13,16 @@
 BIG = -1e30
 MESH = pl.DeviceIdType.MESH
 VMEM = pl.BlockSpec(memory_space=pltpu.VMEM)
-ANY = pl.BlockSpec(memory_space=pl.ANY)
+HBM = pl.BlockSpec(memory_space=pltpu.HBM)
 CHIPS = 32
 GROUP = 8
 QUARTERS = 4
-WITHIN = 6
+DEVICES = 64
+SPREAD, UNSPREAD = 3, 43
+FIRST = 22
+LIMIT = 59 * 2**20
+PAIRS = 8
+MOVES = 8
 SIZE = 512
 
 
@@ -91,7 +96,7 @@
     return jnp.concatenate(out, 1)
 
 
-def gather(part, mine, full, n, local, send_sem, recv_sem, pass_send, pass_recv, where):
+def gather(mine, full, n, send_sem, recv_sem, pass_send, pass_recv, where):
     quarter, g, chip, core, head = where
 
     def block(q, k, i):
@@ -136,88 +141,134 @@
 
 def main_kernel(
     x, w, vclip, aclip, kv, vq, wout,
-    vout, tail, out,
-    xs, ks, vs, qs, os, wt, wl, mine, qkv, hot, mask, mask_t,
+    vout, out,
+    ws, xs, vcs, acs, ks, vs, qs, wos, os, wt, wl, mine, qkv, hot, mask, mask_t,
     sa, sb, ma, mb, numer, stat, near_n, near_s, comb, land, attn, gath, part, swap, back,
-    local, pair_out, one, bar1, bar2, bar3, bar4, bar5, bar6, bar7, bar8,
+    local, pair_out, one, bar1, bar2, bar3, bar4, bar5, bar6,
 ):
     seq, head = lax.axis_index("seq"), lax.axis_index("head")
     chip, core = seq // 2, seq % 2
     quarter, g = chip // GROUP, chip % GROUP
     where = (quarter, g, chip, core, head)
 
-    load_x = pltpu.make_async_copy(x, xs, local.at[0])
-    load_k = pltpu.make_async_copy(kv.at[0], ks, local.at[1])
-    load_v = pltpu.make_async_copy(kv.at[1], vs, local.at[2])
-    load_q = pltpu.make_async_copy(vq, qs, local.at[3])
+    loads = [
+        pltpu.make_async_copy(src, dst, local.at[i])
+        for i, (src, dst) in enumerate(
+            [(w.at[0], ws), (x, xs), (vclip, vcs), (aclip, acs), (kv.at[0], ks),
+             (kv.at[1], vs), (vq, qs), (wout, wos)]
+        )
+    ]
+    load_w, load_x, load_vc, load_ac, load_k, load_v, load_q, load_wo = loads
+    load_w.start()
+    load_vc.start()
+    load_ac.start()
     load_x.start()
 
     barrier = pltpu.get_barrier_semaphore()
 
-    def greet(c, k, h):
-        pl.semaphore_signal(barrier, inc=1, device_id=(c * 2 + k, h), device_id_type=MESH)
-
-    def greet_chip(i, _):
-        greet(lax.rem(chip + i, CHIPS), core, head)
+    def greet(i, _):
+        to = lax.rem(seq + i, DEVICES)
+        pl.semaphore_signal(barrier, inc=1, device_id=(to, head), device_id_type=MESH)
         return 0
 
-    def greet_near(i, _):
-        greet(quarter * GROUP + lax.rem(g + i, GROUP), 1 - core, head)
-        return 0
-
-    lax.fori_loop(0, GROUP, greet_near, 0)
-    lax.fori_loop(1, CHIPS, greet_chip, 0)
-    greet(chip, core, 1 - head)
+    lax.fori_loop(1, DEVICES, greet, 0)
+    pl.semaphore_signal(barrier, inc=1, device_id=(seq, 1 - head), device_id_type=MESH)
     load_k.start()
     load_v.start()
     load_q.start()
-    wt[...] = w[0].astype(F32).T.astype(BF)
-    pl.semaphore_wait(barrier, GROUP + CHIPS)
+    load_wo.start()
+    load_w.wait()
+    wt[...] = ws[...].astype(F32).T.astype(BF)
+    pl.semaphore_wait(barrier, DEVICES)
 
     feature = g * 2 + core
-
-    def weights_to(i):
-        to, k = lax.rem(g + i // 2, GROUP), lax.rem(core + i, 2)
-        rows = wt.at[rows_of((k * GROUP + to) * 48, 48)]
-        return remote(rows, wl.at[feature], one.at[0], one.at[1], quarter * GROUP + to, k, head)
+    mine_at = lax.rem(seq * UNSPREAD, DEVICES)
+    same_quarter = mine_at // 16 == quarter
 
     def weights_start(i, _):
-        weights_to(i).start()
+        b = lax.rem(feature + i, 16)
+        to = lax.rem((quarter * 16 + b) * SPREAD, DEVICES)
+        rows = wt.at[rows_of(b * 48, 48)]
+
+        @pl.when(to == seq)
+        def _():
+            pltpu.make_async_copy(rows, wl.at[feature], one.at[1]).start()
+
+        @pl.when(to != seq)
+        def _():
+            pltpu.make_async_remote_copy(
+                src_ref=rows,
+                dst_ref=wl.at[feature],
+                send_sem=one.at[0],
+                recv_sem=one.at[1],
+                device_id=(to, head),
+                device_id_type=MESH,
+            ).start()
+
         return 0
 
-    own_w = pltpu.make_async_copy(
-        wt.at[rows_of((core * GROUP + g) * 48, 48)], wl.at[feature], one.at[1]
-    )
-    own_w.start()
-    lax.fori_loop(1, 2 * GROUP, weights_start, 0)
-    fill_hot(hot, vclip)
-    flat = clip_mask(aclip)
+    lax.fori_loop(0, 16, weights_start, 0)
+    load_vc.wait()
+    load_ac.wait()
+    fill_hot(hot, vcs)
+    flat = clip_mask(acs)
     mask_t[...] = flat.astype(BF)
     mask[...] = flat.T.astype(BF)
     load_x.wait()
     remote(wl, wl, one.at[0], one.at[1], chip, 1 - core, head).wait_recv()
-    columns = jnp.concatenate([wl[f] for f in range(2 * GROUP)], 1)
+    columns = jnp.concatenate([wl[f] for f in range(16)], 1)
     mine[...] = lax.dot_general(columns, xs[...], NT, preferred_element_type=F32).astype(BF)
 
-    begin, relay, passed, end_first = gather(
-        None, mine, qkv, 48, None, one.at[2], bar1, bar2, bar3, where
-    )
-
-    @pl.when(quarter < 2)
+    has_query = mine_at < FIRST
+    own = qkv.at[rows_of(core * 1536 + mine_at // 2 * 48, 48)]
+    spans = ((0, FIRST // 2 * 48), (FIRST // 2 * 48, (32 - FIRST // 2) * 48))
+
+    def span(p, k):
+        return qkv.at[rows_of(k * 1536 + spans[p][0], spans[p][1])]
+
+    def begin_first(p):
+        pltpu.make_async_copy(mine, own, bar1.at[p]).start()
+
+        def send(i, _):
+            to = lax.rem(chip + i, CHIPS)
+            remote(mine, own, one.at[2], bar1.at[p], to, core, head).start()
+            return 0
+
+        lax.fori_loop(1, CHIPS, send, 0)
+
+    def relay_first(p):
+        remote(span(p, core), span(p, core), one.at[2], bar1.at[p], chip, 1 - core, head).wait_recv()
+        passing(p, core).start()
+
+    def passing(p, k):
+        return remote(span(p, k), span(p, k), bar2.at[p], bar3.at[p], chip, 1 - core, head)
+
+    def end_first():
+        passing(0, core).wait_send()
+        passing(1, core).wait_send()
+        sent = qkv.at[pl.ds(0, (CHIPS - 1) * 48)]
+        remote(sent, sent, one.at[2], bar1.at[0], chip, 1 - core, head).wait_send()
+
+    def rows_at(u):
+        b = u // 3
+        return rows_of(lax.rem(b, 2) * 1536 + b // 2 * 48 + lax.rem(u, 3) * 16, 16)
+
+    def projected(j):
+        return jnp.concatenate([qkv[rows_at(8 * j + t), :] for t in range(8)], 0)
+
+    @pl.when(has_query)
     def _():
-        begin()
-
-    relay(0)
-    relay(1)
-
-    @pl.when(quarter >= 2)
+        begin_first(0)
+
+    relay_first(0)
+
+    @pl.when(jnp.logical_not(has_query))
     def _():
-        begin()
+        begin_first(1)
 
     load_k.wait()
     load_v.wait()
-    passed(0)
-    passed(1)
+    passing(0, 1 - core).wait_recv()
 
     pieces = ks.shape[0] // SIZE
     lane = lax.broadcasted_iota(jnp.int32, (256, 128), 1)
@@ -228,7 +279,7 @@
         return lax.rem(jj + 4 * (1 - core), 8)
 
     def query(jj):
-        q = (qkv[lanes(pair_of(jj)), :].astype(F32) * 0.125).T
+        q = (projected(pair_of(jj)).astype(F32) * 0.125).T
         zero = jnp.zeros_like(q)
         first = jnp.concatenate([jnp.where(lane < 64, q, zero).astype(BF), mask[...]], 1)
         second = jnp.concatenate([jnp.where(lane >= 64, q, zero).astype(BF), mask[...]], 1)
@@ -286,8 +337,7 @@
     send_s = remote(stat.at[0], near_s, one.at[5], one.at[6], chip, 1 - core, head)
     send_n.start()
     send_s.start()
-    relay(2)
-    relay(3)
+    relay_first(1)
     lax.fori_loop(0, 2, functools.partial(two, 1), 0)
 
     send_s.wait_recv()
@@ -319,24 +369,20 @@
     land[0] = comb[chip]
 
     load_q.wait()
-    passed(2)
-    passed(3)
+    load_wo.wait()
+    passing(1, 1 - core).wait_recv()
+
+    def pair_copy(j):
+        return pltpu.make_async_copy(os.at[:, lanes(j)], vout.at[:, lanes(j)], pair_out.at[j])
 
     def video(j0, j1):
         def pair(j, _):
-            video_pair(
-                qkv[lanes(j + 8), :], qkv[lanes(j + 16), :], mask_t[...], hot, qs, os, lanes(j)
-            )
-            pltpu.make_async_copy(
-                os.at[:, lanes(j)], vout.at[:, lanes(j)], pair_out.at[j]
-            ).start()
+            video_pair(projected(j + 8), projected(j + 16), mask_t[...], hot, qs, os, lanes(j))
+            pair_copy(j).start()
             return 0
 
         lax.fori_loop(j0, j1, pair, 0)
 
-    rest = 128 * (8 - WITHIN)
-    tail[:rest, :] = qkv[1024 + 128 * WITHIN : 2048, :]
-    tail[rest:, :] = qkv[2048 + 128 * WITHIN : 3072, :]
     video(0, 3)
 
     others = land.at[pl.ds(1, CHIPS - 1)]
@@ -356,13 +402,13 @@
     attn[...] = (total / scale).astype(BF)
 
     begin, relay, passed, end_second = gather(
-        None, attn, gath, 16, None, one.at[9], bar4, bar5, bar6, where
+        attn, gath, 16, one.at[9], bar4, bar5, bar6, where
     )
     begin()
-    video(3, 5)
+    video(3, 6)
     for q in range(QUARTERS):
         relay(q)
-    video(5, 6)
+    video(6, 7)
     for q in range(QUARTERS):
         passed(q)
     acc = None
@@ -374,7 +420,7 @@
         rows = jnp.concatenate(groups, 0)
         for h in range(2):
             at = k * 512 + h * 256
-            r = lax.dot_general(rows, wout[:, at : at + 256], NT, preferred_element_type=F32)
+            r = lax.dot_general(rows, wos[:, at : at + 256], NT, preferred_element_type=F32)
             r = r.reshape(CHIPS, 16, 32)[:, h * 8 : (h + 1) * 8]
             acc = r if acc is None else acc + r
     flat = acc.reshape(256, 32).T
@@ -382,7 +428,7 @@
     part[1] = flat[:, 128:]
     across = remote(part.at[1 - head], back, one.at[10], one.at[11], chip, core, 1 - head)
     across.start()
-    video(6, WITHIN)
+    video(7, PAIRS)
     across.wait_recv()
     out[...] = (part[head] + back[...]).astype(BF)
 
@@ -392,10 +438,14 @@
     remote(others, others, one.at[7], one.at[8], chip, 1 - core, head).wait_send()
     send_n.wait_send()
     send_s.wait_send()
-    weights = wl.at[pl.ds(0, 2 * GROUP - 1)]
-    remote(weights, weights, one.at[0], one.at[1], chip, 1 - core, head).wait_send()
-    for j in range(WITHIN):
-        pltpu.make_async_copy(os.at[:, lanes(j)], vout.at[:, lanes(j)], pair_out.at[j]).wait()
+    for j in range(PAIRS):
+        pair_copy(j).wait()
+    for count, holds in ((15, same_quarter), (16, jnp.logical_not(same_quarter))):
+
+        @pl.when(holds)
+        def _(count=count):
+            weights = wl.at[pl.ds(0, count)]
+            remote(weights, weights, one.at[0], one.at[1], chip, 1 - core, head).wait_send()
 
 
 def main_part(x, w, vclip, aclip, kv, vq, wout):
@@ -404,18 +454,21 @@
     return pl.pallas_call(
         main_kernel,
         out_shape=(
-            jax.ShapeDtypeStruct((n, 128 * WITHIN), BF),
-            jax.ShapeDtypeStruct((256 * (8 - WITHIN), 256), BF),
+            jax.ShapeDtypeStruct((n, 128 * PAIRS), BF),
             jax.ShapeDtypeStruct((32, 128), BF),
         ),
-        in_specs=[ANY, VMEM, VMEM, VMEM, ANY, ANY, VMEM],
-        out_specs=(ANY, VMEM, VMEM),
+        in_specs=[HBM] * 7,
+        out_specs=(HBM, VMEM),
         scratch_shapes=[
+            pltpu.VMEM((128, 768), BF),
             pltpu.VMEM((256, 2048), BF),
+            pltpu.VMEM((16, 128), jnp.int32),
+            pltpu.VMEM((2, 128), jnp.int32),
             pltpu.VMEM((n, 1024), BF),
             pltpu.VMEM((n, 1024), BF),
             pltpu.VMEM((n, 1024), BF),
-            pltpu.VMEM((n, 128 * WITHIN), BF),
+            pltpu.VMEM((32, 1024), BF),
+            pltpu.VMEM((n, 128 * PAIRS), BF),
             pltpu.VMEM((768, 128), BF),
             pltpu.VMEM((16, 48, 128), BF),
             pltpu.VMEM((48, 256), BF),
@@ -438,66 +491,69 @@
             pltpu.VMEM((2, 32, 128), F32),
             pltpu.VMEM((8, 128), F32),
             pltpu.VMEM((32, 128), F32),
-            dma((4,)),
-            dma((WITHIN,)),
+            dma((8,)),
+            dma((PAIRS,)),
             dma((12,)),
         ]
-        + [dma((QUARTERS,))] * 8,
+        + [dma((QUARTERS,))] * 6,
         compiler_params=pltpu.CompilerParams(
-            collective_id=0, has_side_effects=True, vmem_limit_bytes=52 * 2**20
+            collective_id=0, has_side_effects=True, vmem_limit_bytes=LIMIT
         ),
     )(x, w, vclip, aclip, kv, vq, wout)
 
 
-def tail_kernel(tail, aclip, vclip, vq, first, projected, vout, out, hot, qs, os, sem):
-    move = pltpu.make_async_copy(first, vout.at[:, pl.ds(0, 128 * WITHIN)], sem.at[0])
-    load = pltpu.make_async_copy(
-        vq.at[:, pl.ds(128 * WITHIN, 128 * (8 - WITHIN))], qs, sem.at[1]
-    )
-    load.start()
-    move.start()
-    out[...] = projected[...]
-    fill_hot(hot, vclip)
-    mask_t = clip_mask(aclip).astype(BF)
-    load.wait()
-    rest = 128 * (8 - WITHIN)
-    for j in range(8 - WITHIN):
-        at = slice(j * 128, (j + 1) * 128)
-        keys, values = tail[at, :], tail[rest + j * 128 : rest + (j + 1) * 128, :]
-        video_pair(keys, values, mask_t, hot, qs, os, at)
-        pltpu.make_async_copy(
-            os.at[:, at], vout.at[:, pl.ds(128 * (WITHIN + j), 128)], sem.at[2 + j]
-        ).start()
-    for j in range(8 - WITHIN):
-        at = slice(j * 128, (j + 1) * 128)
-        pltpu.make_async_copy(
-            os.at[:, at], vout.at[:, pl.ds(128 * (WITHIN + j), 128)], sem.at[2 + j]
-        ).wait()
-    move.wait()
-
-
-def tail_part(tail, aclip, vclip, vq, first, projected):
-    n = vq.shape[0]
+def move_kernel(first, projected, vout, out, held, small, read, write, sem):
+    n = first.shape[0] // MOVES
+    fetch = pltpu.make_async_copy(projected, small, sem.at[0])
+    fetch.start()
+
+    def inward(i):
+        rows = pl.ds(i * n, n)
+        return pltpu.make_async_copy(first.at[rows], held.at[rows], read.at[i])
+
+    def outward(i):
+        rows = pl.ds(i * n, n)
+        return pltpu.make_async_copy(held.at[rows], vout.at[rows], write.at[i])
+
+    for i in range(MOVES):
+        inward(i).start()
+    fetch.wait()
+    store = pltpu.make_async_copy(small, out, sem.at[1])
+    store.start()
+    for i in range(MOVES):
+        inward(i).wait()
+        outward(i).start()
+    for i in range(MOVES):
+        outward(i).wait()
+    store.wait()
+
+
+def move_part(first, projected):
+    dma = pltpu.SemaphoreType.DMA
     return pl.pallas_call(
-        tail_kernel,
-        out_shape=(jax.ShapeDtypeStruct(vq.shape, BF), jax.ShapeDtypeStruct((32, 128), BF)),
-        in_specs=[VMEM, VMEM, VMEM, ANY, ANY, VMEM],
-        out_specs=(ANY, VMEM),
+        move_kernel,
+        out_shape=(
+            jax.ShapeDtypeStruct(first.shape, BF),
+            jax.ShapeDtypeStruct(projected.shape, BF),
+        ),
+        in_specs=[HBM, HBM],
+        out_specs=(HBM, HBM),
         scratch_shapes=[
-            pltpu.VMEM((n, 128), BF),
-            pltpu.VMEM((n, 128 * (8 - WITHIN)), BF),
-            pltpu.VMEM((n, 128 * (8 - WITHIN)), BF),
-            pltpu.SemaphoreType.DMA((10 - WITHIN,)),
+            pltpu.VMEM(first.shape, BF),
+            pltpu.VMEM(projected.shape, BF),
+            dma((MOVES,)),
+            dma((MOVES,)),
+            dma((2,)),
         ],
-        compiler_params=pltpu.CompilerParams(vmem_limit_bytes=40 * 2**20),
-    )(tail, aclip, vclip, vq, first, projected)
+        compiler_params=pltpu.CompilerParams(vmem_limit_bytes=LIMIT),
+    )(first, projected)
 
 
 def shards(vq, kv, video_clip, x, w, audio_clip, wout):
     vclip = video_clip.reshape(-1, 128)
     aclip = audio_clip.reshape(-1, 128)
-    first, tail, projected = main_part(x, w, vclip, aclip, kv, vq, wout.T)
-    video_attn, out = tail_part(tail, aclip, vclip, vq, first, projected)
+    first, projected = main_part(x, w, vclip, aclip, kv, vq, wout.T)
+    video_attn, out = move_part(first, projected)
     return video_attn, out.T
 
 

time: 74.9 us -> 63.6 us (0.85)
  local copies, waits for them, and re-layouts: 6.24 us -> 0 us
  Pallas kernels: 67.5 us -> 62.7 us
    unnamed x14 -> x0, local copies, waits for them, and re-layouts: 6.24 us -> none
    pallas_call x2, Pallas kernels: 67.5 us -> 62.7 us  [the longest x1 58.8 us: main_part(): pl.pallas_call(main_kernel, out_shape=(jax.ShapeDtypeStruct((n, 128 * PAI...]
where the time goes in v3:
time: 63.6 us; the launch traced here: 63.5 us
  Pallas kernels  62.7 us (99%)
  between operations  0.8 us (1%)
    pallas_call x1, Pallas kernels, main_part(): pl.pallas_call(main_kernel, out_shape=(jax.ShapeDtypeStruct((n, 128 * PAI...  58.8 us
    pallas_call x1, Pallas kernels, move_part(): pl.pallas_call(move_kernel, out_shape=(jax.ShapeDtypeStruct(first.shape,...  3.96 us

profile of v3, /device:TPU:0, one launch (start us, length us, event | category | flops | bytes accessed | tf_op | source)
XLA Modules:
  0.0 63.5 jit_solution(5602679952363996469)
XLA Ops:
  0.6 58.8 %shard_map.86 = (bf16[2048,1024]{1,0:T(8,128)(2,1)}, bf16[32,128]{1,0:T(8,128)(2,1)}) custom-call(bf16[256,2048]{1,0:T(8,128)(2,1)} %x.1, bf16[1,128,768]{2,1,0:T(8,128)(2,1)} %w.1, s32[16,128]{1,0:T(8,128)} %bitcast.5, s32[2,128]{1,0:T(2,128)} %bitcast.6, bf16[2,2048,1024]{2,1,0:T(8,128)(2,1)} %kv.1, bf16[2048,1024]{1,0:T(8,128)(2,1)} %vq.1, ...), custom_call_target="tpu_custom_call" | custom-call | tf_op jit(solution)/shard_map/pallas_call | solution.py:454
  59.4 4.0 %shard_map.87 = (bf16[2048,1024]{1,0:T(8,128)(2,1)}, bf16[32,128]{1,0:T(8,128)(2,1)}) custom-call(bf16[2048,1024]{1,0:T(8,128)(2,1)} %get-tuple-element.6.first, bf16[32,128]{1,0:T(8,128)(2,1)} %get-tuple-element.7.projected), custom_call_target="tpu_custom_call" | custom-call | tf_op jit(solution)/shard_map/pallas_call | solution.py:533

commit v4 on v3

--- a/solution.py
+++ b/solution.py
@@ -18,8 +18,8 @@
 GROUP = 8
 QUARTERS = 4
 DEVICES = 64
-SPREAD, UNSPREAD = 3, 43
-FIRST = 22
+SPREAD, UNSPREAD = 3, 11
+FIRST = 11
 LIMIT = 59 * 2**20
 PAIRS = 8
 MOVES = 8
@@ -96,60 +96,16 @@
     return jnp.concatenate(out, 1)
 
 
-def gather(mine, full, n, send_sem, recv_sem, pass_send, pass_recv, where):
-    quarter, g, chip, core, head = where
-
-    def block(q, k, i):
-        return full.at[rows_of(((q * 2 + k) * GROUP + i) * n, n)]
-
-    def group(q, k):
-        return full.at[rows_of((q * 2 + k) * GROUP * n, GROUP * n)]
-
-    own = block(quarter, core, g)
-
-    def begin():
-        pltpu.make_async_copy(mine, own, recv_sem.at[quarter]).start()
-
-        def one(i, _):
-            q = lax.rem(quarter + i // GROUP, QUARTERS)
-            to = q * GROUP + lax.rem(g + i, GROUP)
-            remote(mine, own, send_sem, recv_sem.at[quarter], to, core, head).start()
-            return 0
-
-        lax.fori_loop(1, CHIPS, one, 0)
-
-    def relay(q):
-        blocks = group(q, core)
-        remote(blocks, blocks, send_sem, recv_sem.at[q], chip, 1 - core, head).wait_recv()
-        remote(blocks, blocks, pass_send.at[q], pass_recv.at[q], chip, 1 - core, head).start()
-
-    def passed(q):
-        blocks = group(q, 1 - core)
-        remote(blocks, blocks, pass_send.at[q], pass_recv.at[q], chip, 1 - core, head).wait_recv()
-
-    def end():
-        for q in range(QUARTERS):
-            blocks = group(q, core)
-            remote(
-                blocks, blocks, pass_send.at[q], pass_recv.at[q], chip, 1 - core, head
-            ).wait_send()
-        sent = full.at[pl.ds(0, (CHIPS - 1) * n)]
-        remote(sent, sent, send_sem, recv_sem.at[0], chip, 1 - core, head).wait_send()
-
-    return begin, relay, passed, end
-
-
 def main_kernel(
     x, w, vclip, aclip, kv, vq, wout,
     vout, out,
     ws, xs, vcs, acs, ks, vs, qs, wos, os, wt, wl, mine, qkv, hot, mask, mask_t,
-    sa, sb, ma, mb, numer, stat, near_n, near_s, comb, land, attn, gath, part, swap, back,
-    local, pair_out, one, bar1, bar2, bar3, bar4, bar5, bar6,
+    sa, sb, ma, mb, numer, stat, near_n, near_s, comb, land, attn, wide, gath, part, back,
+    local, pair_out, one, bar1, bar2, bar3, bar4, last,
 ):
     seq, head = lax.axis_index("seq"), lax.axis_index("head")
     chip, core = seq // 2, seq % 2
     quarter, g = chip // GROUP, chip % GROUP
-    where = (quarter, g, chip, core, head)
 
     loads = [
         pltpu.make_async_copy(src, dst, local.at[i])
@@ -172,22 +128,32 @@
         return 0
 
     lax.fori_loop(1, DEVICES, greet, 0)
-    pl.semaphore_signal(barrier, inc=1, device_id=(seq, 1 - head), device_id_type=MESH)
+    beside = chip * 2 + 1 - core
+    for to in (seq, beside):
+        pl.semaphore_signal(barrier, inc=1, device_id=(to, 1 - head), device_id_type=MESH)
     load_k.start()
     load_v.start()
     load_q.start()
     load_wo.start()
     load_w.wait()
     wt[...] = ws[...].astype(F32).T.astype(BF)
-    pl.semaphore_wait(barrier, DEVICES)
+    pl.semaphore_wait(barrier, DEVICES + 1)
 
     feature = g * 2 + core
-    mine_at = lax.rem(seq * UNSPREAD, DEVICES)
+    turn = lax.rem((chip + CHIPS - core) * UNSPREAD, CHIPS)
+    late = (turn + CHIPS - FIRST) // CHIPS
+    mine_at = (1 - late) * (FIRST * (1 - core) + turn) + late * (FIRST + 21 * core + turn)
     same_quarter = mine_at // 16 == quarter
+
+    def maker(b):
+        late = (b + DEVICES - 2 * FIRST) // DEVICES
+        k = (1 - late) * (1 - b // FIRST) + late * ((b + 41) // 21 - 3)
+        turn = (1 - late) * (b % FIRST) + late * (FIRST + (b + 41) % 21)
+        return lax.rem(turn * SPREAD + k, CHIPS) * 2 + k
 
     def weights_start(i, _):
         b = lax.rem(feature + i, 16)
-        to = lax.rem((quarter * 16 + b) * SPREAD, DEVICES)
+        to = maker(quarter * 16 + b)
         rows = wt.at[rows_of(b * 48, 48)]
 
         @pl.when(to == seq)
@@ -208,6 +174,13 @@
         return 0
 
     lax.fori_loop(0, 16, weights_start, 0)
+    load_wo.wait()
+    swap_w = remote(
+        wos.at[:, lanes(1 - core, 512)], wide.at[pl.ds(32, 32)], last.at[0], last.at[1],
+        chip, 1 - core, head,
+    )
+    swap_w.start()
+    wide[:32, :] = wos[:, lanes(core, 512)]
     load_vc.wait()
     load_ac.wait()
     fill_hot(hot, vcs)
@@ -219,64 +192,84 @@
     columns = jnp.concatenate([wl[f] for f in range(16)], 1)
     mine[...] = lax.dot_general(columns, xs[...], NT, preferred_element_type=F32).astype(BF)
 
-    has_query = mine_at < FIRST
-    own = qkv.at[rows_of(core * 1536 + mine_at // 2 * 48, 48)]
-    spans = ((0, FIRST // 2 * 48), (FIRST // 2 * 48, (32 - FIRST // 2) * 48))
-
-    def span(p, k):
-        return qkv.at[rows_of(k * 1536 + spans[p][0], spans[p][1])]
-
-    def begin_first(p):
-        pltpu.make_async_copy(mine, own, bar1.at[p]).start()
+    has_query = turn < FIRST
+    own = qkv.at[rows_of(mine_at * 48, 48)]
+
+    def span(k):
+        return qkv.at[rows_of((2 * FIRST + 21 * k) * 48, 21 * 48)]
+
+    def query_block(k, i):
+        return qkv.at[rows_of((FIRST * (1 - k) + i) * 48, 48)]
+
+    def begin_first(sem):
+        pltpu.make_async_copy(mine, own, sem).start()
 
         def send(i, _):
             to = lax.rem(chip + i, CHIPS)
-            remote(mine, own, one.at[2], bar1.at[p], to, core, head).start()
+            remote(mine, own, one.at[2], sem, to, core, head).start()
             return 0
 
         lax.fori_loop(1, CHIPS, send, 0)
 
-    def relay_first(p):
-        remote(span(p, core), span(p, core), one.at[2], bar1.at[p], chip, 1 - core, head).wait_recv()
-        passing(p, core).start()
-
-    def passing(p, k):
-        return remote(span(p, k), span(p, k), bar2.at[p], bar3.at[p], chip, 1 - core, head)
+    def passing_query(k, i):
+        block = query_block(k, i)
+        return remote(block, block, bar2.at[i], bar3.at[i], chip, 1 - core, head)
+
+    def relay_query(n, _):
+        i = lax.rem(n + chip, FIRST)
+        block = query_block(core, i)
+        remote(block, block, one.at[2], bar1.at[i], chip, 1 - core, head).wait_recv()
+        passing_query(core, i).start()
+        return 0
+
+    def query_passed(i, _):
+        passing_query(1 - core, i).wait_recv()
+        return 0
+
+    def passing(k):
+        return remote(span(k), span(k), bar2.at[FIRST], bar3.at[FIRST], chip, 1 - core, head)
+
+    def relay_rest():
+        remote(span(core), span(core), one.at[2], bar1.at[FIRST], chip, 1 - core, head).wait_recv()
+        passing(core).start()
 
     def end_first():
-        passing(0, core).wait_send()
-        passing(1, core).wait_send()
+        def query_sent(i, _):
+            passing_query(core, i).wait_send()
+            return 0
+
+        lax.fori_loop(0, FIRST, query_sent, 0)
+        passing(core).wait_send()
         sent = qkv.at[pl.ds(0, (CHIPS - 1) * 48)]
-        remote(sent, sent, one.at[2], bar1.at[0], chip, 1 - core, head).wait_send()
-
-    def rows_at(u):
-        b = u // 3
-        return rows_of(lax.rem(b, 2) * 1536 + b // 2 * 48 + lax.rem(u, 3) * 16, 16)
+        remote(sent, sent, one.at[2], bar1.at[FIRST], chip, 1 - core, head).wait_send()
 
     def projected(j):
-        return jnp.concatenate([qkv[rows_at(8 * j + t), :] for t in range(8)], 0)
+        return qkv[lanes(j), :]
 
     @pl.when(has_query)
     def _():
-        begin_first(0)
-
-    relay_first(0)
+        begin_first(bar1.at[turn])
+
+    lax.fori_loop(0, FIRST, relay_query, 0)
 
     @pl.when(jnp.logical_not(has_query))
     def _():
-        begin_first(1)
+        begin_first(bar1.at[FIRST])
 
     load_k.wait()
     load_v.wait()
-    passing(0, 1 - core).wait_recv()
 
     pieces = ks.shape[0] // SIZE
     lane = lax.broadcasted_iota(jnp.int32, (256, 128), 1)
     ones = jnp.ones((SIZE, 128), BF)
     stat[...] = jnp.zeros_like(stat)
 
+    def within(jj):
+        return (jj % 4 + (1 - jj // 4) * (1 - core)) % 4
+
     def pair_of(jj):
-        return lax.rem(jj + 4 * (1 - core), 8)
+        half = jj // 4
+        return 4 * ((1 - core) * (1 - half) + core * half) + within(jj)
 
     def query(jj):
         q = (projected(pair_of(jj)).astype(F32) * 0.125).T
@@ -307,16 +300,19 @@
         return r if acc is None else acc + r
 
     def step(jj, half, following, s_ref, m_ref, s_next, m_next):
-        q2 = query(following)
         top, acc, now = None, None, m_ref[...]
+        if following is not None:
+            q2 = query(following)
         for c in range(pieces):
-            top = score(following, q2, c, s_next, top)
+            if following is not None:
+                top = score(following, q2, c, s_next, top)
             acc = weigh(jj, now, c, s_ref, acc)
-        keep(top, m_next)
-        numer[half, :, lanes(jj - 4 * half)] = jnp.where(
+        if following is not None:
+            keep(top, m_next)
+        numer[half, :, lanes(within(jj))] = jnp.where(
             lane < 64, acc[:256, :128], acc[256:, :128]
         )
-        st, at = stat[half], 2 * (jj - 4 * half)
+        st, at = stat[half], 2 * within(jj)
         st = jnp.where(lane == at, now[:256], st)
         st = jnp.where(lane == at + 1, now[256:], st)
         st = jnp.where(lane == at + 64, acc[:256, 128:], st)
@@ -325,7 +321,12 @@
     def two(half, i, _):
         jj = 4 * half + 2 * i
         step(jj, half, jj + 1, sa, ma, sb, mb)
-        step(jj + 1, half, jnp.minimum(jj + 2, 7), sb, mb, sa, ma)
+        step(jj + 1, half, jj + 2, sb, mb, sa, ma)
+
+        @pl.when(jj == 0)
+        def _():
+            lax.fori_loop(0, FIRST, query_passed, 0)
+
         return 0
 
     q2, top = query(0), None
@@ -337,40 +338,53 @@
     send_s = remote(stat.at[0], near_s, one.at[5], one.at[6], chip, 1 - core, head)
     send_n.start()
     send_s.start()
-    relay_first(1)
-    lax.fori_loop(0, 2, functools.partial(two, 1), 0)
+    two(1, 0, 0)
+    step(6, 1, 7, sa, ma, sb, mb)
+    step(7, 1, None, sb, mb, None, None)
+    relay_rest()
 
     send_s.wait_recv()
     send_n.wait_recv()
-    a, b = stat[1], near_s[...]
-    top = jnp.maximum(a, b)
-    high = top.astype(BF).astype(F32)
-    top = high + (top - high).astype(BF).astype(F32)
-    fa = jnp.where(lane < 64, jnp.exp(a - top), 0.0)
-    fb = jnp.where(lane < 64, jnp.exp(b - top), 0.0)
-    st = jnp.where(lane < 64, top, a * pltpu.roll(fa, 64, 1) + b * pltpu.roll(fb, 64, 1))
-    high = st.astype(BF).astype(F32)
-    both = numer[1] * widened(fa, 0, 8) + near_n[...] * widened(fb, 0, 8)
+    narrow = lax.broadcasted_iota(jnp.int32, (64, 128), 1)
 
     def stacked(u, v):
-        return jnp.concatenate(
-            [u.reshape(CHIPS, 8, u.shape[1]), v.reshape(CHIPS, 8, v.shape[1])], 1
-        ).astype(BF)
-
-    comb[:, :, :256] = stacked(both[:, :256], both[:, 256:])
-    comb[:, :, 256:] = stacked(high, st - high)
-
-    def scatter_start(i, _):
-        to = lax.rem(chip + i, CHIPS)
-        remote(comb.at[to], land.at[i], one.at[7], one.at[8], to, core, head).start()
-        return 0
-
-    lax.fori_loop(1, CHIPS, scatter_start, 0)
+        u, v = u.reshape(GROUP, 8, u.shape[1]), v.reshape(GROUP, 8, v.shape[1])
+        return jnp.concatenate([u, v], 1).astype(BF)
+
+    def combine(c, _):
+        base = lax.rem(quarter + 1 + c, QUARTERS) * GROUP
+        rows = rows_of(base * 8, 64)
+        a, b = stat[1, rows, :], near_s[rows, :]
+        top = jnp.maximum(a, b)
+        high = top.astype(BF).astype(F32)
+        top = high + (top - high).astype(BF).astype(F32)
+        fa = jnp.where(narrow < 64, jnp.exp(a - top), 0.0)
+        fb = jnp.where(narrow < 64, jnp.exp(b - top), 0.0)
+        st = jnp.where(narrow < 64, top, a * pltpu.roll(fa, 64, 1) + b * pltpu.roll(fb, 64, 1))
+        high = st.astype(BF).astype(F32)
+        both = numer[1, rows, :] * widened(fa, 0, 8) + near_n[rows, :] * widened(fb, 0, 8)
+        chips = pl.ds(base, GROUP)
+        comb[chips, :, :256] = stacked(both[:, :256], both[:, 256:])
+        comb[chips, :, 256:] = stacked(high, st - high)
+
+        def send(i, _):
+            to = base + lax.rem(g + i, GROUP)
+
+            @pl.when(to != chip)
+            def _():
+                slot = lax.rem(to - chip + CHIPS, CHIPS)
+                remote(comb.at[to], land.at[slot], one.at[7], one.at[8], to, core, head).start()
+
+            return 0
+
+        lax.fori_loop(0, GROUP, send, 0)
+        return 0
+
+    lax.fori_loop(0, QUARTERS, combine, 0)
     land[0] = comb[chip]
 
     load_q.wait()
-    load_wo.wait()
-    passing(1, 1 - core).wait_recv()
+    passing(1 - core).wait_recv()
 
     def pair_copy(j):
         return pltpu.make_async_copy(os.at[:, lanes(j)], vout.at[:, lanes(j)], pair_out.at[j])
@@ -383,7 +397,7 @@
 
         lax.fori_loop(j0, j1, pair, 0)
 
-    video(0, 3)
+    video(0, 4)
 
     others = land.at[pl.ds(1, CHIPS - 1)]
     remote(others, others, one.at[7], one.at[8], chip, 1 - core, head).wait_recv()
@@ -401,40 +415,48 @@
     scale = jnp.concatenate([widened(den, 64, 4), widened(den, 68, 4)], 0)
     attn[...] = (total / scale).astype(BF)
 
-    begin, relay, passed, end_second = gather(
-        attn, gath, 16, one.at[9], bar4, bar5, bar6, where
-    )
-    begin()
-    video(3, 6)
-    for q in range(QUARTERS):
-        relay(q)
-    video(6, 7)
-    for q in range(QUARTERS):
-        passed(q)
+    block = gath.at[rows_of(chip * 16, 16)]
+    pltpu.make_async_copy(attn, block, bar4.at[0]).start()
+
+    def attn_start(i, _):
+        to = lax.rem(chip + i, CHIPS)
+        remote(attn, block, one.at[9], bar4.at[0], to, core, head).start()
+        return 0
+
+    lax.fori_loop(1, CHIPS, attn_start, 0)
+    video(4, 7)
+    remote(gath, gath, one.at[9], bar4.at[0], chip, 1 - core, head).wait_recv()
+    swap_w.wait_recv()
     acc = None
+    for h in range(2):
+        weights = wide[:, h * 256 : (h + 1) * 256]
+        r = lax.dot_general(gath[...], weights, NT, preferred_element_type=F32)
+        r = r.reshape(CHIPS, 16, 64)[:, h * 8 : (h + 1) * 8]
+        acc = r if acc is None else acc + r
+    flat = acc.reshape(256, 64).T
     for k in range(2):
-        groups = [
-            gath[(q * 2 + k) * GROUP * 16 : (q * 2 + k + 1) * GROUP * 16, :]
-            for q in range(QUARTERS)
-        ]
-        rows = jnp.concatenate(groups, 0)
         for h in range(2):
-            at = k * 512 + h * 256
-            r = lax.dot_general(rows, wos[:, at : at + 256], NT, preferred_element_type=F32)
-            r = r.reshape(CHIPS, 16, 32)[:, h * 8 : (h + 1) * 8]
-            acc = r if acc is None else acc + r
-    flat = acc.reshape(256, 32).T
-    part[0] = flat[:, :128]
-    part[1] = flat[:, 128:]
-    across = remote(part.at[1 - head], back, one.at[10], one.at[11], chip, core, 1 - head)
-    across.start()
+            part[k, h] = flat[k * 32 : (k + 1) * 32, h * 128 : (h + 1) * 128]
+    across = [
+        remote(part.at[1, head], back.at[0], last.at[2], last.at[3], chip, 1 - core, head),
+        remote(part.at[0, 1 - head], back.at[1], last.at[4], last.at[5], chip, core, 1 - head),
+        remote(part.at[1, 1 - head], back.at[2], last.at[6], last.at[7], chip, 1 - core, 1 - head),
+    ]
+    for copy in across:
+        copy.start()
     video(7, PAIRS)
-    across.wait_recv()
-    out[...] = (part[head] + back[...]).astype(BF)
-
-    across.wait_send()
+    total = part[0, head]
+    for i, copy in enumerate(across):
+        copy.wait_recv()
+        total = total + back[i]
+    out[...] = total.astype(BF)
+
+    for copy in across:
+        copy.wait_send()
+    swap_w.wait_send()
     end_first()
-    end_second()
+    most = gath.at[pl.ds(0, (CHIPS - 1) * 16)]
+    remote(most, most, one.at[9], bar4.at[0], chip, 1 - core, head).wait_send()
     remote(others, others, one.at[7], one.at[8], chip, 1 - core, head).wait_send()
     send_n.wait_send()
     send_s.wait_send()
@@ -487,15 +509,16 @@
             pltpu.VMEM((CHIPS, 16, 384), BF),
             pltpu.VMEM((CHIPS, 16, 384), BF),
             pltpu.VMEM((16, 256), BF),
-            pltpu.VMEM((1024, 256), BF),
-            pltpu.VMEM((2, 32, 128), F32),
-            pltpu.VMEM((8, 128), F32),
-            pltpu.VMEM((32, 128), F32),
+            pltpu.VMEM((64, 512), BF),
+            pltpu.VMEM((CHIPS * 16, 256), BF),
+            pltpu.VMEM((2, 2, 32, 128), F32),
+            pltpu.VMEM((3, 32, 128), F32),
             dma((8,)),
             dma((PAIRS,)),
             dma((12,)),
         ]
-        + [dma((QUARTERS,))] * 6,
+        + [dma((FIRST + 1,))] * 3
+        + [dma((1,)), dma((8,))],
         compiler_params=pltpu.CompilerParams(
             collective_id=0, has_side_effects=True, vmem_limit_bytes=LIMIT
         ),

time: 63.6 us -> 60.3 us (0.948); the launches traced: 63.5 us -> 59.1 us
  Pallas kernels: 62.7 us -> 58.5 us
    pallas_call x1, Pallas kernels: 58.8 us -> 54.5 us  [main_part(): pl.pallas_call(main_kernel, out_shape=(jax.ShapeDtypeStruct((n, 128 * PAI...]
where the time goes in v4:
time: 60.3 us; the launch traced here: 59.1 us
  Pallas kernels  58.5 us (97%)
  between operations  0.64 us (1%)
    pallas_call x1, Pallas kernels, main_part(): pl.pallas_call(main_kernel, out_shape=(jax.ShapeDtypeStruct((n, 128 * PAI...  54.5 us
    pallas_call x1, Pallas kernels, move_part(): pl.pallas_call(move_kernel, out_shape=(jax.ShapeDtypeStruct(first.shape,...  3.96 us

profile of v4, /device:TPU:0, one launch (start us, length us, event | category | flops | bytes accessed | tf_op | source)
XLA Modules:
  0.0 59.1 jit_solution(9409282195155664824)
XLA Ops:
  0.6 54.5 %shard_map.86 = (bf16[2048,1024]{1,0:T(8,128)(2,1)}, bf16[32,128]{1,0:T(8,128)(2,1)}) custom-call(bf16[256,2048]{1,0:T(8,128)(2,1)} %x.1, bf16[1,128,768]{2,1,0:T(8,128)(2,1)} %w.1, s32[16,128]{1,0:T(8,128)} %bitcast.5, s32[2,128]{1,0:T(2,128)} %bitcast.6, bf16[2,2048,1024]{2,1,0:T(8,128)(2,1)} %kv.1, bf16[2048,1024]{1,0:T(8,128)(2,1)} %vq.1, ...), custom_call_target="tpu_custom_call" | custom-call | tf_op jit(solution)/shard_map/pallas_call | solution.py:476
  55.2 4.0 %shard_map.87 = (bf16[2048,1024]{1,0:T(8,128)(2,1)}, bf16[32,128]{1,0:T(8,128)(2,1)}) custom-call(bf16[2048,1024]{1,0:T(8,128)(2,1)} %get-tuple-element.6.first, bf16[32,128]{1,0:T(8,128)(2,1)} %get-tuple-element.7.projected), custom_call_target="tpu_custom_call" | custom-call | tf_op jit(solution)/shard_map/pallas_call | solution.py:556

commit v5 on v4

--- a/solution.py
+++ b/solution.py
@@ -397,7 +397,7 @@
 
         lax.fori_loop(j0, j1, pair, 0)
 
-    video(0, 4)
+    video(0, 3)
 
     others = land.at[pl.ds(1, CHIPS - 1)]
     remote(others, others, one.at[7], one.at[8], chip, 1 - core, head).wait_recv()
@@ -424,7 +424,7 @@
         return 0
 
     lax.fori_loop(1, CHIPS, attn_start, 0)
-    video(4, 7)
+    video(3, 6)
     remote(gath, gath, one.at[9], bar4.at[0], chip, 1 - core, head).wait_recv()
     swap_w.wait_recv()
     acc = None
@@ -444,7 +444,7 @@
     ]
     for copy in across:
         copy.start()
-    video(7, PAIRS)
+    video(6, PAIRS)
     total = part[0, head]
     for i, copy in enumerate(across):
         copy.wait_recv()

time: 60.3 us -> 59.5 us (0.987)
  Pallas kernels: 58.5 us -> 57.7 us
    pallas_call x1, Pallas kernels: 54.5 us -> 53.8 us  [main_part(): pl.pallas_call(main_kernel, out_shape=(jax.ShapeDtypeStruct((n, 128 * PAI...]
where the time goes in v5:
time: 59.5 us; the launch traced here: 58.4 us
  Pallas kernels  57.7 us (97%)
  between operations  0.64 us (1%)
    pallas_call x1, Pallas kernels, main_part(): pl.pallas_call(main_kernel, out_shape=(jax.ShapeDtypeStruct((n, 128 * PAI...  53.8 us
    pallas_call x1, Pallas kernels, move_part(): pl.pallas_call(move_kernel, out_shape=(jax.ShapeDtypeStruct(first.shape,...  3.96 us

profile of v5, /device:TPU:0, one launch (start us, length us, event | category | flops | bytes accessed | tf_op | source)
XLA Modules:
  0.0 58.4 jit_solution(2690631323482063044)
XLA Ops:
  0.6 53.8 %shard_map.86 = (bf16[2048,1024]{1,0:T(8,128)(2,1)}, bf16[32,128]{1,0:T(8,128)(2,1)}) custom-call(bf16[256,2048]{1,0:T(8,128)(2,1)} %x.1, bf16[1,128,768]{2,1,0:T(8,128)(2,1)} %w.1, s32[16,128]{1,0:T(8,128)} %bitcast.5, s32[2,128]{1,0:T(2,128)} %bitcast.6, bf16[2,2048,1024]{2,1,0:T(8,128)(2,1)} %kv.1, bf16[2048,1024]{1,0:T(8,128)(2,1)} %vq.1, ...), custom_call_target="tpu_custom_call" | custom-call | tf_op jit(solution)/shard_map/pallas_call | solution.py:476
  54.4 4.0 %shard_map.87 = (bf16[2048,1024]{1,0:T(8,128)(2,1)}, bf16[32,128]{1,0:T(8,128)(2,1)}) custom-call(bf16[2048,1024]{1,0:T(8,128)(2,1)} %get-tuple-element.6.first, bf16[32,128]{1,0:T(8,128)(2,1)} %get-tuple-element.7.projected), custom_call_target="tpu_custom_call" | custom-call | tf_op jit(solution)/shard_map/pallas_call | solution.py:556
